TPU v7x, 256 devices: a whole 4x4x8 slice. The times are simulated.
256 devices in a mesh: query: 16 (over x_lo, y, core), tok: 16 (over z, x_hi).
Axes of the slice: x: 4 (x_hi: 2, x_lo: 2; x = x_hi * 2 + x_lo), y: 4, z: 8, core: 2. Of those that a mesh axis runs over, the one named last changes fastest.
Arguments:
- query_acts: bfloat16 [16, 4096, 4096], P('query', 'tok'), may hold values from -6 to 6
- query_grads: bfloat16 [16, 4096, 512], P('query', 'tok'), may hold values from -6 to 6
- sketch_maps: bfloat16 [16, 32, 512], P('query'), may hold values from -0.25 to 0.25
- res_acts: bfloat16 [262144, 4096], P(('query', 'tok')), may hold values from -6 to 6
- res_grads: bfloat16 [262144, 512], P(('query', 'tok')), may hold values from -6 to 6
Outputs:
- scores: float32 [16, 262144], P(None, ('query', 'tok'))
All inputs are finite; a program needn't handle non-finite values.
Results may differ from a plain program's by a relative error of at most 0.0054.
Values may be sent and summed in bfloat16 or wider, within the bound.
No kernel may reach another device: no remote copies, remote signals or barrier semaphores. Data moves between devices by JAX's collectives and lax.ppermute only.
A program may use at most 64 MiB of HBM per device.

v0:
```python
import math

import jax
import jax.numpy as jnp
from jax import lax
from jax.sharding import PartitionSpec as P


def contract_last(first_arr, second_arr):
    return lax.dot_general(
        first_arr, second_arr, (((1,), (1,)), ((), ())), preferred_element_type=jnp.float32
    )


def local(query_acts, query_grads, sketch_maps, res_acts, res_grads):
    local_acts = query_acts[0]
    local_grads = query_grads[0]
    sketch_map = sketch_maps[0]
    rank_count = sketch_map.shape[0]
    projected = contract_last(sketch_map, local_grads).astype(jnp.bfloat16)
    partial_value = jnp.dot(projected, local_acts, preferred_element_type=jnp.float32)
    sketch = lax.psum(partial_value, "tok")
    gram_matrix = jnp.dot(sketch, sketch.T, precision=lax.Precision.HIGHEST)
    lower_factor = jnp.linalg.cholesky(gram_matrix)
    left_factor = lax.linalg.triangular_solve(
        lower_factor, sketch, left_side=True, lower=True
    ).astype(jnp.bfloat16)
    pulled = contract_last(left_factor, local_acts).astype(jnp.bfloat16)
    right_part = jnp.dot(pulled, local_grads, preferred_element_type=jnp.float32)
    right_factor = lax.psum(right_part, "tok").astype(jnp.bfloat16)
    query_count = lax.axis_size("query")
    query_tokens = local_acts.shape[0] * lax.axis_size("tok")
    score_scale = 1.0 / math.sqrt(rank_count * right_factor.shape[1] * query_tokens)
    left_rows = lax.all_gather(left_factor, "query", axis=0, tiled=True)
    rights = lax.all_gather(right_factor, "query", axis=0, tiled=True)
    piece_rows = left_rows.shape[0]
    on_left = contract_last(left_rows, res_acts)
    on_right = contract_last(rights, res_grads)
    product = on_left * on_right
    owners = lax.iota(jnp.int32, piece_rows) // rank_count
    onehot = (owners[None, :] == lax.iota(jnp.int32, query_count)[:, None]).astype(jnp.float32)
    totals = jnp.dot(onehot, product, precision=lax.Precision.HIGHEST)
    return totals * score_scale


def solution(mesh):
    in_specs = (
        P("query", "tok", None),
        P("query", "tok", None),
        P("query", None, None),
        P(("query", "tok"), None),
        P(("query", "tok"), None),
    )
    out_specs = P(None, ("query", "tok"))
    return jax.shard_map(local, mesh=mesh, in_specs=in_specs, out_specs=out_specs, check_vma=False)
```

profile of v0, /device:TPU:32, one launch (start us, length us, event | category | flops | bytes accessed | tf_op | source)
XLA Modules:
  0.0 298.1 jit_solution(12223390314231620420)
XLA Ops:
  6.5 0.0 copy-start
  6.5 0.0 all-reduce.2.cloned.1.call-start
  6.5 1.6 copy-done
  8.1 2.5 fusion.2
  10.7 0.0 copy-start.3
  10.7 0.0 all-reduce.2.cloned.1.call-update
  10.7 0.0 all-gather.2.cloned.1.call-start
  10.7 160.6 %all-reduce.2.cloned.1.call-done = f32[32,4096]{1,0:T(8,128)} async-done(((f32[32,4096]{1,0:T(8,128)}), f32[32,4096]{1,0:T(8,128)}) %all-reduce.2.cloned.1.call-update) | async-done | bytes 524304 | tf_op jit(solution)/shard_map/psum | solution.py:22
  171.3 1.8 fusion.27
  173.1 0.1 copy.6
  173.2 2.9 cholesky.16
  176.1 0.6 compare_reduce_fusion
  176.8 0.7 fusion.20
  177.4 2.4 custom-call.6
  179.9 0.0 copy-start.2
  179.9 2.5 convolution_convert_fusion
  182.4 0.0 all-gather.2.cloned.1.call-update
  182.4 0.0 copy-done.3
  182.4 1.9 fusion.13
  184.3 75.0 %psum.15 = bf16[32,512]{1,0:T(8,128)(2,1)S(1)} all-reduce(f32[32,512]{1,0:T(8,128)S(1)} %fusion.13), channel_id=1, replica_groups=mesh['query'=16,'tok'=16] {'tok'}, use_global_device_ids=true, to_apply=%region_3.4 | all-reduce | flops 16384 | bytes 98304 | tf_op jit(solution)/shard_map/psum | solution.py:30
  259.3 20.0 %all_gather.7 = bf16[512,512]{1,0:T(8,128)(2,1)S(1)} all-gather(bf16[32,512]{1,0:T(8,128)(2,1)S(1)} %psum.15), channel_id=1, replica_groups=mesh['query'=16,'tok'=16] {'query'}, dimensions={0}, use_global_device_ids=true | all-gather | bytes 557056 | tf_op jit(solution)/shard_map/all_gather | solution.py:35
  279.3 0.0 copy-done.2
  279.3 2.1 fusion.29
  281.4 0.0 all-gather.2.cloned.1.call-done
  281.4 0.0 copy-start.1
  281.4 8.3 %fusion.28 = f32[512,1024]{1,0:T(8,128)S(1)} fusion(bf16[512,4096]{1,0:T(8,128)(2,1)} %all-gather.2.cloned.1.call-done, bf16[1024,4096]{1,0:T(8,128)(2,1)} %param.8), kind=kOutput, calls=%fused_computation.33 | convolution fusion | flops 4294967296 | bytes 14680064 | tf_op jit(solution)/shard_map/dot_general | solution.py:10
  289.7 0.0 copy-done.1
  289.8 1.5 fusion.6
  (3 shorter events, 0.0 us)
Async XLA Ops:
  6.5 1.6 copy-start
  6.5 164.8 %all-reduce.2.cloned.1.call-start = ((), (), s32[]{:S(2)}) async-start(), calls=%async_computation | async-start | bytes 1048576 | tf_op jit(solution)/shard_map/psum | solution.py:22
  10.7 171.8 %copy-start.3 = (bf16[1,256,512]{2,1,0:T(8,128)(2,1)S(1)}, bf16[1,256,512]{2,1,0:T(8,128)(2,1)}, u32[]{:S(2)}) copy-start(bf16[1,256,512]{2,1,0:T(8,128)(2,1)} %param.6) | copy-start | bytes 786436
  10.7 270.7 %all-gather.2.cloned.1.call-start = ((), (), s32[]{:S(2)}) async-start(), calls=%async_computation.1 | async-start | bytes 4456448 | tf_op jit(solution)/shard_map/all_gather | solution.py:34
  179.9 99.4 %copy-start.2 = (bf16[1024,512]{1,0:T(8,128)(2,1)S(1)}, bf16[1024,512]{1,0:T(8,128)(2,1)}, u32[]{:S(2)}) copy-start(bf16[1024,512]{1,0:T(8,128)(2,1)} %param.9) | copy-start | bytes 3145732
  281.4 8.4 %copy-start.1 = (f32[512,1024]{1,0:T(8,128)S(1)}, f32[512,1024]{1,0:T(8,128)}, u32[]{:S(2)}) copy-start(f32[512,1024]{1,0:T(8,128)} %fusion.29) | copy-start | bytes 6291460
Sparse Core Ops, SparseCore 0:
  10.8 160.5 all-reduce.1
  182.5 38.5 all-gather.1
where the time goes:
time: 302 us; the launch traced here: 298 us
  waiting for transfers between devices  161 us (53%)
  blocking collectives  95 us (31%)
  matrix products  20.6 us (7%)
  between operations  13.5 us (4%)
  other arithmetic  6.69 us (2%)
    psum x1, waiting for transfers between devices, local(): sketch = lax.psum(partial_value, 'tok')  161 us
    psum x1, blocking collectives, local(): right_factor = lax.psum(right_part, 'tok').astype(jnp.bfloat16)  75 us
    all_gather x1, blocking collectives, local(): rights = lax.all_gather(right_factor, 'query', axis=0, tiled=True)  20 us
    dot_general x2, matrix products, contract_last(): lax.dot_general(first_arr, second_arr, (((1,), (1,)), ((), ())), preferre...  10.4 us
  transfers between devices with their start and end apart: 2, of which 1 were waited for; matrix products, arithmetic and copies ran while one was open for 1% of the time, Pallas kernels for 0%

commit v1 on v0

v1 whole, which is shorter than its diff:
```python
import math

import jax
import jax.numpy as jnp
from jax import lax
from jax.sharding import Mesh
from jax.sharding import PartitionSpec as P

QUERY = ("xlo", "y", "core")
TOK = ("z", "xhi")
HIGH = lax.Precision.HIGHEST
F32 = jnp.float32
BF16 = jnp.bfloat16


def contract_last(first_arr, second_arr):
    return lax.dot_general(first_arr, second_arr, (((1,), (1,)), ((), ())), preferred_element_type=F32)


def exchange(blocks, axes):
    return lax.all_to_all(blocks, axes, 0, 0, tiled=True)


def spread(block, axes, count):
    return exchange(jnp.broadcast_to(block[None], (count,) + block.shape), axes)


def local(query_acts, query_grads, sketch_maps, res_acts, res_grads):
    acts, grads, sketch_map = query_acts[0], query_grads[0], sketch_maps[0]
    rank, width = sketch_map.shape[0], acts.shape[1]
    groups = lax.axis_size(TOK)
    queries = lax.axis_size(QUERY)
    part = width // groups
    score_scale = 1.0 / math.sqrt(rank * grads.shape[1] * acts.shape[0] * groups)

    projected = contract_last(sketch_map, grads).astype(BF16)
    partial = jnp.dot(projected, acts, preferred_element_type=F32).astype(BF16)
    partial = partial.reshape(rank, groups, part).transpose(1, 0, 2)
    piece = jnp.sum(exchange(partial, TOK).astype(F32), axis=0).astype(BF16)
    sketch = spread(piece, TOK, groups).transpose(1, 0, 2).reshape(rank, width)

    pulled = contract_last(sketch, acts).astype(BF16)
    right_part = jnp.dot(pulled, grads, preferred_element_type=F32).astype(BF16)
    right_parts = spread(right_part, TOK, groups)

    lefts = lax.all_gather(sketch, QUERY, axis=0, tiled=True)
    on_left = contract_last(lefts, res_acts)

    lower = jnp.linalg.cholesky(contract_last(sketch, sketch))
    inverse = lax.linalg.triangular_solve(lower, jnp.eye(rank, dtype=F32), left_side=True, lower=True)
    right = jnp.sum(right_parts.astype(F32), axis=0)
    right = jnp.dot(inverse.T, jnp.dot(inverse, right, precision=HIGH), precision=HIGH)
    rights = spread(right.astype(BF16), QUERY, queries).reshape(queries * rank, -1)
    on_right = contract_last(rights, res_grads)
    product = (on_left * on_right).reshape(queries, rank, -1)
    return jnp.sum(product, axis=1) * score_scale


def solution(mesh):
    fine = Mesh(mesh.devices.reshape(2, 4, 2, 8, 2), QUERY + TOK)
    in_specs = (
        P(QUERY, TOK, None),
        P(QUERY, TOK, None),
        P(QUERY, None, None),
        P(QUERY + TOK, None),
        P(QUERY + TOK, None),
    )
    return jax.shard_map(local, mesh=fine, in_specs=in_specs, out_specs=P(None, QUERY + TOK), check_vma=False)
```

time: 302 us -> 116 us (0.38)
  waiting for transfers between devices: 161 us -> 23.3 us
  blocking collectives: 95 us -> 38.2 us
  starting transfers between devices: 0.04 us -> 9.57 us
    psum x1 -> x0, waiting for transfers between devices: 161 us -> none  [local(): sketch = lax.psum(partial_value, 'tok')]
    psum x1 -> x0, blocking collectives: 75 us -> none  [local(): right_factor = lax.psum(right_part, 'tok').astype(jnp.bfloat16)]
    all_to_all x0 -> x2, blocking collectives: none -> 38.2 us  [exchange(): return lax.all_to_all(blocks, axes, 0, 0, tiled=True)]
    all_gather x1 -> x0, blocking collectives: 20 us -> none  [local(): rights = lax.all_gather(right_factor, 'query', axis=0, tiled=True)]
    all_gather x1, waiting for transfers between devices: 0.01 us -> 15.8 us  [local(): lefts = lax.all_gather(sketch, QUERY, axis=0, tiled=True)]
    all_to_all x0 -> x2, starting transfers between devices: none -> 9.57 us  [exchange(): return lax.all_to_all(blocks, axes, 0, 0, tiled=True)]
    all_to_all x0 -> x2, waiting for transfers between devices: none -> 7.54 us  [exchange(): return lax.all_to_all(blocks, axes, 0, 0, tiled=True)]
    dot_general x4, matrix products: 7.65 us -> 4.03 us  [the longest x1 1.88 us: local(): right_part = jnp.dot(pulled, grads, preferred_element_type=F32).astype(BF16)]
  transfers between devices with their start and end apart: 2 -> 3, of which waited for: 1 -> 2; matrix products, arithmetic and copies ran while one was open for 1% -> 19% of each run, Pallas kernels for 0% -> 0%
where the time goes in v1:
time: 116 us; the launch traced here: 114 us
  blocking collectives  38.2 us (33%)
  waiting for transfers between devices  23.3 us (20%)
  matrix products  17.6 us (15%)
  between operations  13.5 us (12%)
  starting transfers between devices  9.57 us (8%)
  other arithmetic  7.45 us (6%)
  local copies, waits for them, and re-layouts  4.16 us (4%)
    all_to_all x2, blocking collectives, exchange(): return lax.all_to_all(blocks, axes, 0, 0, tiled=True)  38.2 us
    all_gather x1, waiting for transfers between devices, local(): lefts = lax.all_gather(sketch, QUERY, axis=0, tiled=True)  15.8 us
    dot_general x3, matrix products, contract_last(): lax.dot_general(first_arr, second_arr, (((1,), (1,)), ((), ())), preferre...  13.4 us
    all_to_all x2, starting transfers between devices, exchange(): return lax.all_to_all(blocks, axes, 0, 0, tiled=True)  9.57 us
    all_to_all x2, waiting for transfers between devices, exchange(): return lax.all_to_all(blocks, axes, 0, 0, tiled=True)  7.54 us
    another operation x3, other arithmetic, local(): lower = jnp.linalg.cholesky(contract_last(sketch, sketch))  3.6 us
    another operation x2, other arithmetic, local(): lax.linalg.triangular_solve(lower, jnp.eye(rank, dtype=F32), left_side=Tr...  3.09 us
  transfers between devices with their start and end apart: 3, of which 2 were waited for; matrix products, arithmetic and copies ran while one was open for 19% of the time, Pallas kernels for 0%

profile of v1, /device:TPU:32, one launch (start us, length us, event | category | flops | bytes accessed | tf_op | source)
XLA Modules:
  0.0 113.9 jit_solution(10483839300001098773)
XLA Ops:
  6.5 0.0 copy-start
  6.5 0.0 all-gather.2.cloned.1.call-start
  6.5 1.6 %copy-done = bf16[1,256,4096]{2,1,0:T(8,128)(2,1)S(1)} copy-done((bf16[1,256,4096]{2,1,0:T(8,128)(2,1)S(1)}, bf16[1,256,4096]{2,1,0:T(8,128)(2,1)}, u32[]{:S(2)}) %copy-start) | copy-done | bytes 2097176
  8.1 1.7 %convolution_convert_fusion = bf16[32,4096]{1,0:T(8,128)(2,1)S(1)} fusion(bf16[1,256,4096]{2,1,0:T(8,128)(2,1)S(1)} %copy-done, bf16[1,256,512]{2,1,0:T(8,128)(2,1)} %param.6, bf16[1,32,512]{2,1,0:T(8,128)(2,1)} %param.7), kind=kOutput, calls=%fused_computation | convolution fusion | flops 75636736 | bytes 2654208 | tf_op jit(solution)/shard_map/dot_general | solution.py:37
  9.8 0.0 copy-start.1
  9.9 23.1 %all_to_all.20 = bf16[16,32,256]{2,1,0:T(8,128)(2,1)S(1)} all-to-all(bf16[16,32,256]{2,1,0:T(8,128)(2,1)S(1)} %bitcast.58), channel_id=1, replica_groups=mesh['xlo'=2,'y'=4,'core'=2,'z'=8,'xhi'=2] {'z','xhi'}, dimensions={0} | all-to-all | bytes 524288 | tf_op jit(solution)/shard_map/all_to_all | solution.py:21
  33.0 15.1 %all_to_all.21 = bf16[16,32,256]{2,1,0:T(8,128)(2,1)S(1)} all-to-all(bf16[16,32,256]{2,1,0:T(8,128)(2,1)S(1)} %broadcast_in_dim.7), channel_id=1, replica_groups=mesh['xlo'=2,'y'=4,'core'=2,'z'=8,'xhi'=2] {'z','xhi'}, dimensions={0} | all-to-all | bytes 524288 | tf_op jit(solution)/shard_map/all_to_all | solution.py:21
  48.2 0.7 copy.16
  48.9 0.0 all-gather.2.cloned.1.call-update
  48.9 0.0 copy-done.1
  48.9 1.9 %convolution_convert_fusion.2 = bf16[32,512]{1,0:T(8,128)(2,1)S(1)} fusion(bf16[32,4096]{1,0:T(8,128)(2,1)} %bitcast.55, bf16[1,256,4096]{2,1,0:T(8,128)(2,1)S(1)} %copy-done, bf16[1,256,512]{2,1,0:T(8,128)(2,1)S(1)} %copy-done.1), kind=kOutput, calls=%fused_computation.7 | convolution fusion | flops 75522048 | bytes 2654208 | tf_op jit(solution)/shard_map/dot_general | solution.py:43
  50.8 0.9 broadcast_in_dim.8
  51.7 5.0 %all-to-all-start.2 = ((bf16[16,32,512]{2,1,0:T(8,128)(2,1)}), bf16[16,32,512]{2,1,0:T(8,128)(2,1)S(1)}, u32[]{:S(2)}, u32[]{:S(2)}) async-start(bf16[16,32,512]{2,1,0:T(8,128)(2,1)} %broadcast_in_dim.8), calls=%async_computation.2 | async-start | bytes 1048576 | tf_op jit(solution)/shard_map/all_to_all | solution.py:21
  56.7 0.2 convolution_bitcast_fusion
  56.9 0.1 copy.14
  57.0 2.9 %cholesky.17 = f32[32,32]{1,0:T(8,128)S(1)} custom-call(f32[32,32]{1,0:T(8,128)S(1)} %fusion.17), custom_call_target="Cholesky" | custom-call | tf_op jit(solution)/shard_map/jit(cholesky)/cholesky | solution.py:49
  59.9 0.6 compare_reduce_fusion
  60.6 0.7 fusion.14
  61.2 2.4 %custom-call.6 = f32[1,32,32]{1,2,0:T(8,128)S(1)} custom-call(f32[1,32,32]{2,1,0:T(8,128)S(1)} %fusion.14), custom_call_target="InvertDiagBlocksLowerTriangular" | custom-call | tf_op jit(solution)/shard_map/triangular_solve | solution.py:50
  63.7 0.2 fusion.15
  63.9 7.5 %all-to-all-done.2 = bf16[16,32,512]{2,1,0:T(8,128)(2,1)S(1)} async-done(((bf16[16,32,512]{2,1,0:T(8,128)(2,1)}), bf16[16,32,512]{2,1,0:T(8,128)(2,1)S(1)}, u32[]{:S(2)}, u32[]{:S(2)}) %all-to-all-start.2) | async-done | bytes 524320 | tf_op jit(solution)/shard_map/all_to_all | solution.py:21
  71.4 0.1 convert_reduce_fusion
  71.5 0.2 fusion.19
  71.7 0.3 convolution_convert_fusion.1
  72.0 0.9 broadcast_in_dim.10
  72.8 4.6 %all-to-all-start.3 = ((bf16[16,32,512]{2,1,0:T(8,128)(2,1)}), bf16[16,32,512]{2,1,0:T(8,128)(2,1)S(1)}, u32[]{:S(2)}, u32[]{:S(2)}) async-start(bf16[16,32,512]{2,1,0:T(8,128)(2,1)} %broadcast_in_dim.10), calls=%async_computation.3 | async-start | bytes 1048576 | tf_op jit(solution)/shard_map/all_to_all | solution.py:21
  77.4 15.8 %all-gather.2.cloned.1.call-done = bf16[512,4096]{1,0:T(8,128)(2,1)} async-done(((bf16[32,4096]{1,0:T(8,128)(2,1)}), bf16[512,4096]{1,0:T(8,128)(2,1)}) %all-gather.2.cloned.1.call-update) | async-done | bytes 4194320 | tf_op jit(solution)/shard_map/all_gather | solution.py:46
  93.2 10.5 %fusion.18 = f32[512,1024]{1,0:T(8,128)} fusion(bf16[512,4096]{1,0:T(8,128)(2,1)} %all-gather.2.cloned.1.call-done, bf16[1024,4096]{1,0:T(8,128)(2,1)} %param.8), kind=kOutput, calls=%fused_computation.28 | convolution fusion | flops 4294967296 | bytes 14680064 | tf_op jit(solution)/shard_map/dot_general | solution.py:17
  103.7 0.0 all-to-all-done.3
  103.7 2.7 %bitcast_reduce_fusion = f32[16,1024]{1,0:T(8,128)S(1)} fusion(f32[512,1024]{1,0:T(8,128)} %fusion.18, bf16[512,512]{1,0:T(8,128)(2,1)S(1)} %bitcast.56, bf16[1024,512]{1,0:T(8,128)(2,1)} %param.9), kind=kOutput, calls=%fused_computation.1 | convolution fusion | flops 537903104 | bytes 3735552 | tf_op jit(solution)/shard_map/dot_general | solution.py:17
  106.4 0.6 broadcast_multiply_fusion
  (5 shorter events, 0.1 us)
Async XLA Ops:
  6.5 1.6 %copy-start = (bf16[1,256,4096]{2,1,0:T(8,128)(2,1)S(1)}, bf16[1,256,4096]{2,1,0:T(8,128)(2,1)}, u32[]{:S(2)}) copy-start(bf16[1,256,4096]{2,1,0:T(8,128)(2,1)} %param.5) | copy-start | bytes 6291460
  6.5 86.6 %all-gather.2.cloned.1.call-start = ((), (), s32[]{:S(2)}) async-start(), calls=%async_computation.4 | async-start | bytes 4456448 | tf_op jit(solution)/shard_map/all_gather | solution.py:46
  9.8 39.1 %copy-start.1 = (bf16[1,256,512]{2,1,0:T(8,128)(2,1)S(1)}, bf16[1,256,512]{2,1,0:T(8,128)(2,1)}, u32[]{:S(2)}) copy-start(bf16[1,256,512]{2,1,0:T(8,128)(2,1)} %param.6) | copy-start | bytes 786436
  51.7 19.7 %all-to-all-start.2 = ((bf16[16,32,512]{2,1,0:T(8,128)(2,1)}), bf16[16,32,512]{2,1,0:T(8,128)(2,1)S(1)}, u32[]{:S(2)}, u32[]{:S(2)}) async-start(bf16[16,32,512]{2,1,0:T(8,128)(2,1)} %broadcast_in_dim.8), calls=%async_computation.2 | async-start | bytes 1048576 | tf_op jit(solution)/shard_map/all_to_all | solution.py:21
  72.8 30.9 %all-to-all-start.3 = ((bf16[16,32,512]{2,1,0:T(8,128)(2,1)}), bf16[16,32,512]{2,1,0:T(8,128)(2,1)S(1)}, u32[]{:S(2)}, u32[]{:S(2)}) async-start(bf16[16,32,512]{2,1,0:T(8,128)(2,1)} %broadcast_in_dim.10), calls=%async_computation.3 | async-start | bytes 1048576 | tf_op jit(solution)/shard_map/all_to_all | solution.py:21
Sparse Core Ops, SparseCore 0:
  49.1 44.0 all-gather.1

commit v2 on v1

v2 whole, which is shorter than its diff:
```python
import math

import jax
import jax.numpy as jnp
from jax import lax
from jax.experimental import pallas as pl
from jax.experimental.pallas import tpu as pltpu
from jax.sharding import Mesh
from jax.sharding import PartitionSpec as P

QUERY = ("xlo", "y", "core")
TOK = ("z", "xhi")
HIGH = lax.Precision.HIGHEST
F32 = jnp.float32
BF16 = jnp.bfloat16
VMEM_LIMIT = 28 * 2**20
STREAM_LIMIT = 60 * 2**20
PIECES = 4


def contract_last(first_arr, second_arr):
    return lax.dot_general(first_arr, second_arr, (((1,), (1,)), ((), ())), preferred_element_type=F32)


def params():
    return pltpu.CompilerParams(dimension_semantics=("arbitrary",), vmem_limit_bytes=VMEM_LIMIT)


def cost(flops, num_bytes):
    return pl.CostEstimate(flops=flops, bytes_accessed=num_bytes, transcendentals=0)


def exchange(blocks, axes):
    return lax.all_to_all(blocks, axes, 0, 0, tiled=True)


def swap_cores(block):
    return lax.ppermute(block, "core", [(0, 1), (1, 0)])


def partial_sketch(sketch_maps, query_grads, query_acts, groups):
    projected = contract_last(sketch_maps[0], query_grads[0]).astype(BF16)
    partial = jnp.dot(projected, query_acts[0], preferred_element_type=F32).astype(BF16)
    rank, width = partial.shape
    return partial.reshape(rank, groups, width // groups).transpose(1, 0, 2)


def piece_kernel(parts_ref, out_ref):
    total = jnp.sum(parts_ref[...].astype(F32), axis=0).astype(BF16)
    out_ref[...] = jnp.broadcast_to(total[None], out_ref.shape)


def sum_pieces(parts):
    return pl.pallas_call(
        piece_kernel,
        out_shape=jax.ShapeDtypeStruct(parts.shape, BF16),
        compiler_params=pltpu.CompilerParams(vmem_limit_bytes=VMEM_LIMIT),
    )(parts)


def right_kernel(sketch_ref, acts_ref, grads_ref, out_ref, gram_ref, pulled_ref):
    step = pl.program_id(0)
    blocks, _, part = sketch_ref.shape

    @pl.when(step == 0)
    def _():
        pulled_ref[...] = jnp.zeros_like(pulled_ref)
        gram_ref[...] = jnp.zeros_like(gram_ref)

    for i in range(blocks):
        block = sketch_ref[i]
        pulled_ref[...] += contract_last(acts_ref[0, :, i * part : (i + 1) * part], block)
        gram_ref[...] += contract_last(block, block)

    @pl.when(step == pl.num_programs(0) - 1)
    def _():
        pulled = pulled_ref[...].T.astype(BF16)
        right = jnp.dot(pulled, grads_ref[0], preferred_element_type=F32)
        out_ref[...] = jnp.broadcast_to(right.astype(BF16)[None], out_ref.shape)


def partial_right(sketch, query_acts, query_grads):
    groups, rank, part = sketch.shape
    _, tokens, width = query_acts.shape
    outs = query_grads.shape[2]
    steps = 4
    return pl.pallas_call(
        right_kernel,
        grid=(steps,),
        in_specs=[
            pl.BlockSpec((groups // steps, rank, part), lambda i: (i, 0, 0)),
            pl.BlockSpec((1, tokens, width // steps), lambda i: (0, 0, i)),
            pl.BlockSpec((1, tokens, outs), lambda i: (0, 0, 0)),
        ],
        out_specs=[
            pl.BlockSpec((groups, rank, outs), lambda i: (0, 0, 0)),
            pl.BlockSpec((rank, rank), lambda i: (0, 0)),
        ],
        out_shape=[
            jax.ShapeDtypeStruct((groups, rank, outs), BF16),
            jax.ShapeDtypeStruct((rank, rank), F32),
        ],
        scratch_shapes=[pltpu.VMEM((tokens, rank), F32)],
        compiler_params=params(),
        cost_estimate=cost(2 * rank * tokens * (width + outs), 2 * tokens * (width + outs)),
    )(sketch, query_acts, query_grads)


def solve_kernel(parts_ref, inverse_ref, out_ref):
    total = jnp.sum(parts_ref[...].astype(F32), axis=0)
    inverse = inverse_ref[...]
    half = jnp.dot(inverse, total, precision=HIGH, preferred_element_type=F32)
    full = lax.dot_general(inverse, half, (((0,), (0,)), ((), ())), precision=HIGH, preferred_element_type=F32)
    out_ref[...] = jnp.broadcast_to(full.astype(BF16)[None], out_ref.shape)


def solve_right(parts, inverse, queries):
    _, rank, outs = parts.shape
    return pl.pallas_call(
        solve_kernel,
        out_shape=jax.ShapeDtypeStruct((queries, rank, outs), BF16),
        compiler_params=pltpu.CompilerParams(vmem_limit_bytes=VMEM_LIMIT),
    )(parts, inverse)


def stack_rows(near_ref, far_ref):
    chips, blocks, rank, part = near_ref.shape

    def rows(i):
        return jnp.concatenate([ref[:, i].reshape(chips * rank, part) for ref in (near_ref, far_ref)], axis=0)

    return jnp.concatenate([rows(i) for i in range(blocks)], axis=1)


def row_copies(acts_ref, held_ref, sems):
    pieces, height, _ = held_ref.shape
    return [
        pltpu.make_async_copy(acts_ref.at[pl.ds(i * height, height)], held_ref.at[i], sems.at[i])
        for i in range(pieces)
    ]


def row_scratch(res_acts):
    tokens, width = res_acts.shape
    return [pltpu.VMEM((PIECES, tokens // PIECES, width), BF16), pltpu.SemaphoreType.DMA((PIECES,))]


def whole_copies(refs, held_refs, sems):
    return [pltpu.make_async_copy(ref, held, sems.at[i]) for i, (ref, held) in enumerate(zip(refs, held_refs))]


def whole_scratch(*arrays):
    return [pltpu.VMEM(x.shape, x.dtype) for x in arrays] + [pltpu.SemaphoreType.DMA((len(arrays),))]


def left_kernel(near_ref, far_ref, acts_ref, out_ref, held_ref, sems, near_held_ref, far_held_ref, pair_sems):
    pair = whole_copies((near_ref, far_ref), (near_held_ref, far_held_ref), pair_sems)
    copies = row_copies(acts_ref, held_ref, sems)
    for copy in pair + copies:
        copy.start()
    for copy in pair:
        copy.wait()
    rows = stack_rows(near_held_ref, far_held_ref)
    height = held_ref.shape[1]
    for i, copy in enumerate(copies):
        copy.wait()
        out_ref[i * height : (i + 1) * height] = contract_last(held_ref[i], rows)


def on_left(near, far, res_acts):
    rows, tokens = 2 * near.shape[0] * near.shape[2], res_acts.shape[0]
    return pl.pallas_call(
        left_kernel,
        in_specs=[pl.BlockSpec(memory_space=pl.ANY)] * 3,
        out_specs=pl.BlockSpec(memory_space=pltpu.VMEM),
        out_shape=jax.ShapeDtypeStruct((tokens, rows), F32),
        scratch_shapes=row_scratch(res_acts) + whole_scratch(near, far),
        compiler_params=pltpu.CompilerParams(vmem_limit_bytes=STREAM_LIMIT),
        cost_estimate=cost(0, 0),
    )(near, far, res_acts)


def sum_ranks(product, queries, rank):
    shape = (queries, queries * rank)
    owner = lax.broadcasted_iota(jnp.int32, shape, 1) // rank
    chosen = (owner == lax.broadcasted_iota(jnp.int32, shape, 0)).astype(BF16)
    total = 0.0
    for _ in range(3):
        term = product.astype(BF16)
        total = total + contract_last(chosen, term)
        product = product - term.astype(F32)
    return total


def make_score_kernel(score_scale):
    def score_kernel(order_ref, *refs):
        (near_ref, far_ref, own_ref, rights_ref, grads_ref, acts_ref, out_ref), refs = refs[:7], refs[7:]
        (held_ref, sems, sorted_ref, near_held_ref, far_held_ref, own_held_ref, rights_held_ref, grads_held_ref), refs = (
            refs[:8],
            refs[8:],
        )
        near_copy, far_copy, own_copy, rights_copy, grads_copy = whole_copies(
            (near_ref, far_ref, own_ref, rights_ref, grads_ref),
            (near_held_ref, far_held_ref, own_held_ref, rights_held_ref, grads_held_ref),
            refs[0],
        )
        copies = row_copies(acts_ref, held_ref, sems)
        for copy in [rights_copy, grads_copy, near_copy, far_copy] + copies + [own_copy]:
            copy.start()

        queries, rank, outs = rights_ref.shape
        half = queries // 2
        height = held_ref.shape[1]
        rights_copy.wait()
        for i in range(queries):
            sorted_ref[i] = rights_held_ref[order_ref[i]]
        grads_copy.wait()
        on_right = contract_last(grads_held_ref[...], sorted_ref[...].reshape(queries * rank, outs))

        near_copy.wait()
        far_copy.wait()
        rows = stack_rows(near_held_ref, far_held_ref)
        for j, copy in enumerate(copies):
            copy.wait()
            tokens = slice(j * height, (j + 1) * height)
            product = contract_last(held_ref[j], rows) * on_right[tokens, half * rank :]
            other = sum_ranks(product, half, rank) * score_scale
            for i in range(half):
                out_ref[pl.ds(order_ref[half + i], 1), tokens] = other[i : i + 1]

        own_copy.wait()
        own = sum_ranks(own_held_ref[...] * on_right[:, : half * rank], half, rank) * score_scale
        for i in range(half):
            out_ref[pl.ds(order_ref[i], 1), :] = own[i : i + 1]

    return score_kernel


def all_scores(order, near, far, res_acts, own, rights, res_grads, score_scale):
    tokens, rows = own.shape
    queries = rights.shape[0]
    return pl.pallas_call(
        make_score_kernel(score_scale),
        in_specs=[pl.BlockSpec(memory_space=pltpu.SMEM)] + [pl.BlockSpec(memory_space=pl.ANY)] * 6,
        out_specs=pl.BlockSpec(memory_space=pltpu.VMEM),
        out_shape=jax.ShapeDtypeStruct((queries, tokens), F32),
        scratch_shapes=row_scratch(res_acts)
        + [pltpu.VMEM(rights.shape, BF16)]
        + whole_scratch(near, far, own, rights, res_grads),
        compiler_params=pltpu.CompilerParams(vmem_limit_bytes=STREAM_LIMIT),
        cost_estimate=cost(2 * rows * (res_acts.size + 2 * res_grads.size), 2 * res_acts.size),
    )(order, near, far, own, rights, res_grads, res_acts)


def from_back(block, axis, step):
    size = lax.axis_size(axis)
    return lax.ppermute(block, axis, [(i, (i + step) % size) for i in range(size)])


NEAR = ((0, 0), (1, 0), (0, 1), (0, 3))
FAR = ((1, 1), (1, 3), (0, 2), (1, 2))


def local(query_acts, query_grads, sketch_maps, res_acts, res_grads):
    rank, outs = sketch_maps.shape[1:]
    groups, queries = lax.axis_size(TOK), lax.axis_size(QUERY)
    score_scale = 1.0 / math.sqrt(rank * outs * query_acts.shape[1] * groups)

    parts = exchange(partial_sketch(sketch_maps, query_grads, query_acts, groups), TOK)
    sketch = exchange(sum_pieces(parts), TOK)
    right_part, gram = partial_right(sketch, query_acts, query_grads)
    sketch, right_part = lax.optimization_barrier((sketch, right_part))
    right_parts = exchange(right_part, TOK)

    lower = jnp.linalg.cholesky(gram)
    inverse = lax.linalg.triangular_solve(lower, jnp.eye(rank, dtype=F32), left_side=True, lower=True)
    right = solve_right(right_parts, inverse, queries)

    rights = exchange(right, QUERY)

    beside = from_back(sketch, "xlo", 1)
    behind, ahead = from_back(sketch, "y", 1), from_back(sketch, "y", 3)
    near = jnp.stack([sketch, beside, behind, ahead])
    other_near = swap_cores(near)
    corners = [from_back(beside, "y", 1), from_back(beside, "y", 3)]
    across = [from_back(behind, "y", 1), from_back(corners[1], "y", 3)]
    _, corners, across = lax.optimization_barrier((right, corners, across))
    far = jnp.stack(corners + across)
    other_far = swap_cores(far)

    wide, high = lax.axis_size("xlo"), lax.axis_size("y")
    column, row = lax.axis_index("xlo"), lax.axis_index("y")
    place = [(column + wide - x) % wide * high + (row + high - y) % high for x, y in NEAR + FAR]
    place = 2 * jnp.stack(place).astype(jnp.int32)
    core = lax.axis_index("core").astype(jnp.int32)
    order = jnp.concatenate([place + core, place + 1 - core])

    own_left = on_left(near, far, res_acts)
    return all_scores(order, other_near, other_far, res_acts, own_left, rights, res_grads, score_scale)


def solution(mesh):
    fine = Mesh(mesh.devices.reshape(2, 4, 2, 8, 2), QUERY + TOK)
    in_specs = (
        P(QUERY, TOK, None),
        P(QUERY, TOK, None),
        P(QUERY, None, None),
        P(QUERY + TOK, None),
        P(QUERY + TOK, None),
    )
    return jax.shard_map(local, mesh=fine, in_specs=in_specs, out_specs=P(None, QUERY + TOK), check_vma=False)
```

time: 116 us -> 104 us (0.90)
  Pallas kernels: 0 us -> 25 us
  waiting for transfers between devices: 23.3 us -> 5.98 us
  matrix products: 17.6 us -> 2.6 us
  between operations: 13.5 us -> 0.39 us
  starting transfers between devices: 9.57 us -> 19.7 us
  local copies, waits for them, and re-layouts: 4.16 us -> 1.79 us
    pallas_call x0 -> x5, Pallas kernels: none -> 25 us  [the longest x1 11.4 us: all_scores(): pl.pallas_call(make_score_kernel(score_scale), in_specs=[pl.BlockSpec(mem...]
    all_gather x1 -> x0, waiting for transfers between devices: 15.8 us -> none  [local(): lefts = lax.all_gather(sketch, QUERY, axis=0, tiled=True)]
    dot_general x7 -> x1, matrix products: 17.4 us -> 2.41 us  [partial_sketch(): jnp.dot(projected, query_acts[0], preferred_element_type=F32).astype(BF16)]
    ppermute x0 -> x9, starting transfers between devices: none -> 10.9 us  [the longest x7 10.7 us: from_back(): lax.ppermute(block, axis, [(i, (i + step) % size) for i in range(size)])]
    all_to_all x2, waiting for transfers between devices: 7.54 us -> 0.29 us  [exchange(): return lax.all_to_all(blocks, axes, 0, 0, tiled=True)]
    ppermute x0 -> x9, waiting for transfers between devices: none -> 5.68 us  [the longest x7 5.68 us: from_back(): lax.ppermute(block, axis, [(i, (i + step) % size) for i in range(size)])]
    broadcast_in_dim x3 -> x0, local copies, waits for them, and re-layouts: 1.75 us -> none  [spread(): return exchange(jnp.broadcast_to(block[None], (count,) + block.shape), axes)]
    another operation x3 -> x5, other arithmetic: 3.6 us -> 4.88 us  [the longest x3 3.58 us: local(): lower = jnp.linalg.cholesky(gram)]
  transfers between devices with their start and end apart: 3 -> 11, of which waited for: 2 -> 3; matrix products, arithmetic and copies ran while one was open for 19% -> 9% of each run, Pallas kernels for 0% -> 11%
where the time goes in v2:
time: 104 us; the launch traced here: 102 us
  blocking collectives  38.1 us (37%)
  Pallas kernels  25 us (24%)
  starting transfers between devices  19.7 us (19%)
  other arithmetic  8.58 us (8%)
  waiting for transfers between devices  5.98 us (6%)
  matrix products  2.6 us (2%)
  local copies, waits for them, and re-layouts  1.79 us (2%)
    all_to_all x2, blocking collectives, exchange(): return lax.all_to_all(blocks, axes, 0, 0, tiled=True)  38.1 us
    pallas_call x1, Pallas kernels, all_scores(): pl.pallas_call(make_score_kernel(score_scale), in_specs=[pl.BlockSpec(mem...  11.4 us
    ppermute x7, starting transfers between devices, from_back(): lax.ppermute(block, axis, [(i, (i + step) % size) for i in range(size)])  10.7 us
    pallas_call x1, Pallas kernels, on_left(): pl.pallas_call(left_kernel, in_specs=[pl.BlockSpec(memory_space=pl.ANY)]...  9.58 us
    all_to_all x2, starting transfers between devices, exchange(): return lax.all_to_all(blocks, axes, 0, 0, tiled=True)  8.77 us
    ppermute x7, waiting for transfers between devices, from_back(): lax.ppermute(block, axis, [(i, (i + step) % size) for i in range(size)])  5.68 us
    another operation x3, other arithmetic, local(): lower = jnp.linalg.cholesky(gram)  3.58 us
    another operation x2, other arithmetic, local(): lax.linalg.triangular_solve(lower, jnp.eye(rank, dtype=F32), left_side=Tr...  3.09 us
  transfers between devices with their start and end apart: 11, of which 3 were waited for; matrix products, arithmetic and copies ran while one was open for 9% of the time, Pallas kernels for 11%

profile of v2, /device:TPU:32, one launch (start us, length us, event | category | flops | bytes accessed | tf_op | source)
XLA Modules:
  0.0 102.1 jit_solution(10658349491357431954)
XLA Ops:
  0.0 0.7 copy-done
  0.8 2.4 %convolution_convert_fusion = bf16[32,4096]{1,0:T(8,128)(2,1)S(1)} fusion(bf16[1,256,4096]{2,1,0:T(8,128)(2,1)} %acts_ref.2, bf16[1,256,512]{2,1,0:T(8,128)(2,1)} %grads_ref.1, bf16[1,32,512]{2,1,0:T(8,128)(2,1)S(1)} %copy-done), kind=kOutput, calls=%fused_computation | convolution fusion | flops 75636736 | bytes 2654208 | tf_op jit(solution)/shard_map/dot_general | solution.py:43
  3.2 23.0 %all_to_all.20.parts_ref = bf16[16,32,256]{2,1,0:T(8,128)(2,1)S(1)} all-to-all(bf16[16,32,256]{2,1,0:T(8,128)(2,1)S(1)} %bitcast.44), channel_id=1, replica_groups=mesh['xlo'=2,'y'=4,'core'=2,'z'=8,'xhi'=2] {'z','xhi'}, dimensions={0} | all-to-all | bytes 524288 | tf_op jit(solution)/shard_map/all_to_all | solution.py:34
  26.2 15.1 %all_to_all.21.sketch_ref = bf16[16,32,256]{2,1,0:T(8,128)(2,1)S(1)} all-to-all(bf16[16,32,256]{2,1,0:T(8,128)(2,1)S(1)} %shard_map.55), channel_id=1, replica_groups=mesh['xlo'=2,'y'=4,'core'=2,'z'=8,'xhi'=2] {'z','xhi'}, dimensions={0} | all-to-all | bytes 524288 | tf_op jit(solution)/shard_map/all_to_all | solution.py:34
  41.4 2.6 %shard_map.56 = (bf16[16,32,512]{2,1,0:T(8,128)(2,1)}, f32[32,32]{1,0:T(8,128)S(1)}) custom-call(bf16[16,32,256]{2,1,0:T(8,128)(2,1)S(1)} %all_to_all.21.sketch_ref, bf16[1,256,4096]{2,1,0:T(8,128)(2,1)S(1)} %copy-done.1, bf16[1,256,512]{2,1,0:T(8,128)(2,1)S(1)} %copy-done.2), custom_call_target="tpu_custom_call" | custom-call | flops 75497472 | bytes 2359296 | tf_op jit(solution)/shard_map/pallas_call | solution.py:87
  44.0 3.0 %collective-permute-start.2 = (bf16[16,32,256]{2,1,0:T(8,128)(2,1)S(1)}, bf16[16,32,256]{2,1,0:T(8,128)(2,1)S(1)}, u32[]{:S(2)}, u32[]{:S(2)}) collective-permute-start(bf16[16,32,256]{2,1,0:T(8,128)(2,1)S(1)} %all_to_all.21.sketch_ref), channel_id=1, source_target_pairs={{0,96},{32,0},{64,32},{96,64},{1,97},{33,1},{65,33},{97,65},{2,98}... | collective-permute-start | bytes 786440 | tf_op jit(solution)/shard_map/ppermute | solution.py:257
  47.0 0.6 collective-permute-start
  47.6 5.0 %all-to-all-start.2 = ((bf16[16,32,512]{2,1,0:T(8,128)(2,1)}), bf16[16,32,512]{2,1,0:T(8,128)(2,1)S(1)}, u32[]{:S(2)}, u32[]{:S(2)}) async-start(bf16[16,32,512]{2,1,0:T(8,128)(2,1)} %get-tuple-element.15), calls=%async_computation.2 | async-start | bytes 1048576 | tf_op jit(solution)/shard_map/all_to_all | solution.py:34
  52.6 0.1 copy.8
  52.7 2.9 %cholesky.17 = f32[32,32]{1,0:T(8,128)S(1)} custom-call(f32[32,32]{1,0:T(8,128)S(1)} %fusion.8), custom_call_target="Cholesky" | custom-call | tf_op jit(solution)/shard_map/jit(cholesky)/cholesky | solution.py:275
  55.6 3.3 %collective-permute-start.5 = (bf16[16,32,256]{2,1,0:T(8,128)(2,1)S(1)}, bf16[16,32,256]{2,1,0:T(8,128)(2,1)S(1)}, u32[]{:S(2)}, u32[]{:S(2)}) collective-permute-start(bf16[16,32,256]{2,1,0:T(8,128)(2,1)S(1)} %collective-permute-done), channel_id=1, source_target_pairs={{0,96},{32,0},{64,32},{96,64},{1,97},{33,1},{65,33},{97,65},{2,98}... | collective-permute-start | bytes 786440 | tf_op jit(solution)/shard_map/ppermute | solution.py:257
  59.0 0.6 compare_reduce_fusion
  59.6 0.7 fusion.5
  60.2 2.4 %custom-call.6 = f32[1,32,32]{1,2,0:T(8,128)S(1)} custom-call(f32[1,32,32]{2,1,0:T(8,128)S(1)} %fusion.5), custom_call_target="InvertDiagBlocksLowerTriangular" | custom-call | tf_op jit(solution)/shard_map/triangular_solve | solution.py:276
  62.7 0.0 collective-permute-start.4
  62.7 0.1 collective-permute-start.6
  62.8 0.6 collective-permute-done.5
  63.4 3.7 %collective-permute-start.7 = (bf16[16,32,256]{2,1,0:T(8,128)(2,1)S(1)}, bf16[16,32,256]{2,1,0:T(8,128)(2,1)}, u32[]{:S(2)}, u32[]{:S(2)}) collective-permute-start(bf16[16,32,256]{2,1,0:T(8,128)(2,1)S(1)} %collective-permute-done.5), channel_id=1, source_target_pairs={{0,96},{32,0},{64,32},{96,64},{1,97},{33,1},{65,33},{97,65},{2,98}... | collective-permute-start | bytes 786440 | tf_op jit(solution)/shard_map/ppermute | solution.py:257
  67.1 0.2 fusion.6.inverse_ref
  67.3 0.1 pad_maximum_fusion.near_ref
  67.5 0.1 collective-permute-start.3
  67.6 1.3 %shard_map.57 = bf16[16,32,512]{2,1,0:T(8,128)(2,1)} custom-call(bf16[16,32,512]{2,1,0:T(8,128)(2,1)S(1)} %all-to-all-done.2.parts_ref, f32[32,32]{1,0:T(8,128)S(1)} %fusion.6.inverse_ref), custom_call_target="tpu_custom_call" | custom-call | tf_op jit(solution)/shard_map/pallas_call | solution.py:119
  68.9 5.1 %collective-permute-done.6 = bf16[16,32,256]{2,1,0:T(8,128)(2,1)} collective-permute-done((bf16[16,32,256]{2,1,0:T(8,128)(2,1)S(1)}, bf16[16,32,256]{2,1,0:T(8,128)(2,1)}, u32[]{:S(2)}, u32[]{:S(2)}) %collective-permute-start.6) | collective-permute-done | bytes 262176 | tf_op jit(solution)/shard_map/ppermute | solution.py:257
  74.0 1.2 %pad_maximum_fusion.1.far_ref = bf16[4,16,32,256]{3,2,1,0:T(8,128)(2,1)S(1)} fusion(bf16[1,16,32,256]{3,2,1,0:T(8,128)(2,1)} %bitcast.22, bf16[1,16,32,256]{3,2,1,0:T(8,128)(2,1)} %bitcast.21, bf16[1,16,32,256]{3,2,1,0:T(8,128)(2,1)S(1)} %bitcast.49, bf16[1,16,32,256]{3,2,1,0:T(8,128)(2,1)S(1)} %bitcast.50), kind=kLoop, calls=%fused_computation.4 | loop fusion | flops 1572864 | bytes 2097152 | tf_op jit(solution)/shard_map/stack | solution.py:288
  75.2 0.1 collective-permute-start.8
  75.3 3.8 %all-to-all-start.3 = ((bf16[16,32,512]{2,1,0:T(8,128)(2,1)}), bf16[16,32,512]{2,1,0:T(8,128)(2,1)S(1)}, u32[]{:S(2)}, u32[]{:S(2)}) async-start(bf16[16,32,512]{2,1,0:T(8,128)(2,1)} %shard_map.57), calls=%async_computation.3 | async-start | bytes 1048576 | tf_op jit(solution)/shard_map/all_to_all | solution.py:34
  79.1 0.1 stack.65
  79.2 0.6 pad_add_fusion.order_ref
  79.8 9.6 %shard_map.58.refs_2_ = f32[1024,256]{1,0:T(8,128)} custom-call(bf16[4,16,32,256]{3,2,1,0:T(8,128)(2,1)} %copy-done.3, bf16[4,16,32,256]{3,2,1,0:T(8,128)(2,1)} %copy-done.4, bf16[1024,4096]{1,0:T(8,128)(2,1)} %refs_5_.1), custom_call_target="tpu_custom_call" | custom-call | tf_op jit(solution)/shard_map/pallas_call | solution.py:172
  89.4 0.3 all-to-all-done.3.refs_3_
  89.7 0.8 copy-done.5
  90.5 11.4 %shard_map.59 = f32[16,1024]{1,0:T(8,128)} custom-call(s32[16]{0:T(128)} %pad_add_fusion.order_ref, bf16[4,16,32,256]{3,2,1,0:T(8,128)(2,1)} %collective-permute-done.3.refs_0_, bf16[4,16,32,256]{3,2,1,0:T(8,128)(2,1)} %collective-permute-done.8.refs_1_, f32[1024,256]{1,0:T(8,128)} %shard_map.58.refs_2_, bf16[16,32,512]{2,1,0:T(8,128)(2,1)} %copy-done.5, ...), custom_call_target="tpu_custom_call" | custom-call | flops 2684354560 | bytes 8388608 | tf_op jit(solution)/shard_map/pallas_call | solution.py:242
  (24 shorter events, 0.2 us)
Async XLA Ops:
  0.0 0.8 copy-start
  0.0 41.4 %copy-start.2 = (bf16[1,256,512]{2,1,0:T(8,128)(2,1)S(1)}, bf16[1,256,512]{2,1,0:T(8,128)(2,1)}, u32[]{:S(2)}) copy-start(bf16[1,256,512]{2,1,0:T(8,128)(2,1)} %grads_ref.1) | copy-start | bytes 786436
  0.0 41.4 %copy-start.1 = (bf16[1,256,4096]{2,1,0:T(8,128)(2,1)S(1)}, bf16[1,256,4096]{2,1,0:T(8,128)(2,1)}, u32[]{:S(2)}) copy-start(bf16[1,256,4096]{2,1,0:T(8,128)(2,1)} %acts_ref.2) | copy-start | bytes 6291460
  44.0 23.3 %collective-permute-start.2 = (bf16[16,32,256]{2,1,0:T(8,128)(2,1)S(1)}, bf16[16,32,256]{2,1,0:T(8,128)(2,1)S(1)}, u32[]{:S(2)}, u32[]{:S(2)}) collective-permute-start(bf16[16,32,256]{2,1,0:T(8,128)(2,1)S(1)} %all_to_all.21.sketch_ref), channel_id=1, source_target_pairs={{0,96},{32,0},{64,32},{96,64},{1,97},{33,1},{65,33},{97,65},{2,98}... | collective-permute-start | bytes 786440 | tf_op jit(solution)/shard_map/ppermute | solution.py:257
  47.0 15.7 %collective-permute-start.1 = (bf16[16,32,256]{2,1,0:T(8,128)(2,1)S(1)}, bf16[16,32,256]{2,1,0:T(8,128)(2,1)S(1)}, u32[]{:S(2)}, u32[]{:S(2)}) collective-permute-start(bf16[16,32,256]{2,1,0:T(8,128)(2,1)S(1)} %all_to_all.21.sketch_ref), channel_id=1, source_target_pairs={{0,32},{32,64},{64,96},{96,0},{1,33},{33,65},{65,97},{97,1},{2,34}... | collective-permute-start | bytes 786440 | tf_op jit(solution)/shard_map/ppermute | solution.py:257
  47.0 8.6 %collective-permute-start = (bf16[16,32,256]{2,1,0:T(8,128)(2,1)S(1)}, bf16[16,32,256]{2,1,0:T(8,128)(2,1)S(1)}, u32[]{:S(2)}, u32[]{:S(2)}) collective-permute-start(bf16[16,32,256]{2,1,0:T(8,128)(2,1)S(1)} %all_to_all.21.sketch_ref), channel_id=1, source_target_pairs={{0,128},{128,0},{1,129},{129,1},{2,130},{130,2},{3,131},{131,3},{4... | collective-permute-start | bytes 786440 | tf_op jit(solution)/shard_map/ppermute | solution.py:257
  47.6 20.0 %all-to-all-start.2 = ((bf16[16,32,512]{2,1,0:T(8,128)(2,1)}), bf16[16,32,512]{2,1,0:T(8,128)(2,1)S(1)}, u32[]{:S(2)}, u32[]{:S(2)}) async-start(bf16[16,32,512]{2,1,0:T(8,128)(2,1)} %get-tuple-element.15), calls=%async_computation.2 | async-start | bytes 1048576 | tf_op jit(solution)/shard_map/all_to_all | solution.py:34
  55.6 7.8 %collective-permute-start.5 = (bf16[16,32,256]{2,1,0:T(8,128)(2,1)S(1)}, bf16[16,32,256]{2,1,0:T(8,128)(2,1)S(1)}, u32[]{:S(2)}, u32[]{:S(2)}) collective-permute-start(bf16[16,32,256]{2,1,0:T(8,128)(2,1)S(1)} %collective-permute-done), channel_id=1, source_target_pairs={{0,96},{32,0},{64,32},{96,64},{1,97},{33,1},{65,33},{97,65},{2,98}... | collective-permute-start | bytes 786440 | tf_op jit(solution)/shard_map/ppermute | solution.py:257
  62.7 11.3 %collective-permute-start.4 = (bf16[16,32,256]{2,1,0:T(8,128)(2,1)S(1)}, bf16[16,32,256]{2,1,0:T(8,128)(2,1)S(1)}, u32[]{:S(2)}, u32[]{:S(2)}) collective-permute-start(bf16[16,32,256]{2,1,0:T(8,128)(2,1)S(1)} %collective-permute-done), channel_id=1, source_target_pairs={{0,32},{32,64},{64,96},{96,0},{1,33},{33,65},{65,97},{97,1},{2,34}... | collective-permute-start | bytes 786440 | tf_op jit(solution)/shard_map/ppermute | solution.py:257
  62.7 11.2 %collective-permute-start.6 = (bf16[16,32,256]{2,1,0:T(8,128)(2,1)S(1)}, bf16[16,32,256]{2,1,0:T(8,128)(2,1)}, u32[]{:S(2)}, u32[]{:S(2)}) collective-permute-start(bf16[16,32,256]{2,1,0:T(8,128)(2,1)S(1)} %collective-permute-done.1), channel_id=1, source_target_pairs={{0,32},{32,64},{64,96},{96,0},{1,33},{33,65},{65,97},{97,1},{2,34}... | collective-permute-start | bytes 786440 | tf_op jit(solution)/shard_map/ppermute | solution.py:257
  63.4 10.6 %collective-permute-start.7 = (bf16[16,32,256]{2,1,0:T(8,128)(2,1)S(1)}, bf16[16,32,256]{2,1,0:T(8,128)(2,1)}, u32[]{:S(2)}, u32[]{:S(2)}) collective-permute-start(bf16[16,32,256]{2,1,0:T(8,128)(2,1)S(1)} %collective-permute-done.5), channel_id=1, source_target_pairs={{0,96},{32,0},{64,32},{96,64},{1,97},{33,1},{65,33},{97,65},{2,98}... | collective-permute-start | bytes 786440 | tf_op jit(solution)/shard_map/ppermute | solution.py:257
  67.5 7.8 %copy-start.3 = (bf16[4,16,32,256]{3,2,1,0:T(8,128)(2,1)}, bf16[4,16,32,256]{3,2,1,0:T(8,128)(2,1)S(1)}, u32[]{:S(2)}) copy-start(bf16[4,16,32,256]{3,2,1,0:T(8,128)(2,1)S(1)} %pad_maximum_fusion.near_ref) | copy-start | bytes 3145732
  67.5 21.9 %collective-permute-start.3 = (bf16[4,16,32,256]{3,2,1,0:T(8,128)(2,1)S(1)}, bf16[4,16,32,256]{3,2,1,0:T(8,128)(2,1)}, u32[]{:S(2)}, u32[]{:S(2)}) collective-permute-start(bf16[4,16,32,256]{3,2,1,0:T(8,128)(2,1)S(1)} %pad_maximum_fusion.near_ref), channel_id=1, source_target_pairs={{0,16},{16,0},{1,17},{17,1},{2,18},{18,2},{3,19},{19,3},{4,20},{20... | collective-permute-start | bytes 3145736 | tf_op jit(solution)/shard_map/ppermute | solution.py:38
  75.2 4.7 %copy-start.4 = (bf16[4,16,32,256]{3,2,1,0:T(8,128)(2,1)}, bf16[4,16,32,256]{3,2,1,0:T(8,128)(2,1)S(1)}, u32[]{:S(2)}) copy-start(bf16[4,16,32,256]{3,2,1,0:T(8,128)(2,1)S(1)} %pad_maximum_fusion.1.far_ref) | copy-start | bytes 3145732
  75.2 14.5 %collective-permute-start.8 = (bf16[4,16,32,256]{3,2,1,0:T(8,128)(2,1)S(1)}, bf16[4,16,32,256]{3,2,1,0:T(8,128)(2,1)}, u32[]{:S(2)}, u32[]{:S(2)}) collective-permute-start(bf16[4,16,32,256]{3,2,1,0:T(8,128)(2,1)S(1)} %pad_maximum_fusion.1.far_ref), channel_id=1, source_target_pairs={{0,16},{16,0},{1,17},{17,1},{2,18},{18,2},{3,19},{19,3},{4,20},{20... | collective-permute-start | bytes 3145736 | tf_op jit(solution)/shard_map/ppermute | solution.py:38
  75.3 14.4 %all-to-all-start.3 = ((bf16[16,32,512]{2,1,0:T(8,128)(2,1)}), bf16[16,32,512]{2,1,0:T(8,128)(2,1)S(1)}, u32[]{:S(2)}, u32[]{:S(2)}) async-start(bf16[16,32,512]{2,1,0:T(8,128)(2,1)} %shard_map.57), calls=%async_computation.3 | async-start | bytes 1048576 | tf_op jit(solution)/shard_map/all_to_all | solution.py:34
  89.7 0.8 copy-start.5

commit v3 on v1

v3 whole, which is shorter than its diff:
```python
import math

import jax
import jax.numpy as jnp
from jax import lax
from jax.experimental import pallas as pl
from jax.experimental.pallas import tpu as pltpu
from jax.sharding import Mesh
from jax.sharding import PartitionSpec as P

QUERY = ("xlo", "y", "core")
TOK = ("z", "xhi")
HIGH = lax.Precision.HIGHEST
F32 = jnp.float32
BF16 = jnp.bfloat16
VMEM_LIMIT = 12 * 2**20


def contract_last(first_arr, second_arr):
    return lax.dot_general(first_arr, second_arr, (((1,), (1,)), ((), ())), preferred_element_type=F32)


def cost(flops, num_bytes):
    return pl.CostEstimate(flops=flops, bytes_accessed=num_bytes, transcendentals=0)


def exchange(blocks, axes):
    return lax.all_to_all(blocks, axes, 0, 0, tiled=True)


def swap_cores(block):
    return lax.ppermute(block, "core", [(0, 1), (1, 0)])


def stack_rows(refs):
    blocks = range(refs[0].shape[0])
    return jnp.concatenate([jnp.concatenate([ref[i] for ref in refs], axis=0) for i in blocks], axis=1)


def partial_sketch(sketch_maps, query_grads, query_acts, groups):
    projected = contract_last(sketch_maps[0], query_grads[0]).astype(BF16)
    partial = jnp.dot(projected, query_acts[0], preferred_element_type=F32).astype(BF16)
    rank, width = partial.shape
    return partial.reshape(rank, groups, width // groups).transpose(1, 0, 2)


def piece_kernel(parts_ref, out_ref):
    total = jnp.sum(parts_ref[...].astype(F32), axis=0).astype(BF16)
    out_ref[...] = jnp.broadcast_to(total[None], out_ref.shape)


def sum_pieces(parts):
    return pl.pallas_call(
        piece_kernel,
        out_shape=jax.ShapeDtypeStruct(parts.shape, BF16),
        compiler_params=pltpu.CompilerParams(vmem_limit_bytes=VMEM_LIMIT),
    )(parts)


def right_kernel(sketch_ref, acts_ref, grads_ref, out_ref, gram_ref):
    sketch = stack_rows([sketch_ref])
    pulled = contract_last(acts_ref[0], sketch)
    gram_ref[...] = contract_last(sketch, sketch)
    right = jnp.dot(pulled.T.astype(BF16), grads_ref[0], preferred_element_type=F32)
    out_ref[...] = jnp.broadcast_to(right.astype(BF16)[None], out_ref.shape)


def partial_right(sketch, query_acts, query_grads):
    groups, rank, _ = sketch.shape
    outs = query_grads.shape[2]
    vmem = pl.BlockSpec(memory_space=pltpu.VMEM)
    return pl.pallas_call(
        right_kernel,
        in_specs=[vmem] * 3,
        out_specs=[vmem] * 2,
        out_shape=[
            jax.ShapeDtypeStruct((groups, rank, outs), BF16),
            jax.ShapeDtypeStruct((rank, rank), F32),
        ],
        compiler_params=pltpu.CompilerParams(vmem_limit_bytes=VMEM_LIMIT),
        cost_estimate=cost(2 * rank * (query_acts.size + query_grads.size), 2 * query_acts.size),
    )(sketch, query_acts, query_grads)


def inverse_kernel(gram_ref, out_ref):
    rank = gram_ref.shape[0]
    row = lax.broadcasted_iota(jnp.int32, (rank, 2 * rank), 0)
    column = lax.broadcasted_iota(jnp.int32, (rank, 2 * rank), 1)
    unit = (column - rank == row).astype(F32)
    pair = jnp.concatenate([gram_ref[...], unit[:, rank:]], axis=1)
    for i in range(rank):
        pivot = pair[i : i + 1] / pair[i : i + 1, i : i + 1]
        pair = jnp.where(row == i, pivot, pair - pair[:, i : i + 1] * pivot)
    out_ref[...] = pair[:, rank:]


def invert(gram):
    return pl.pallas_call(
        inverse_kernel,
        out_shape=jax.ShapeDtypeStruct(gram.shape, F32),
        compiler_params=pltpu.CompilerParams(vmem_limit_bytes=VMEM_LIMIT),
        cost_estimate=cost(2**32, 2**22),
    )(gram)


def solve_kernel(parts_ref, inverse_ref, out_ref):
    total = jnp.sum(parts_ref[...].astype(F32), axis=0)
    out_ref[...] = jnp.dot(inverse_ref[...], total, precision=HIGH, preferred_element_type=F32).astype(BF16)


def solve_right(parts, inverse):
    return pl.pallas_call(
        solve_kernel,
        out_shape=jax.ShapeDtypeStruct(parts.shape[1:], BF16),
        compiler_params=pltpu.CompilerParams(vmem_limit_bytes=VMEM_LIMIT),
        cost_estimate=cost(0, 0),
    )(parts, inverse)


def touch_kernel(acts_ref, out_ref):
    out_ref[...] = acts_ref[: out_ref.shape[0], : out_ref.shape[1]]


def touch(res_acts):
    vmem = pl.BlockSpec(memory_space=pltpu.VMEM)
    return pl.pallas_call(
        touch_kernel,
        in_specs=[vmem],
        out_specs=vmem,
        out_shape=jax.ShapeDtypeStruct((16, 128), res_acts.dtype),
        compiler_params=pltpu.CompilerParams(vmem_limit_bytes=VMEM_LIMIT),
        cost_estimate=cost(0, 2 * res_acts.size),
    )(res_acts)


def left_kernel(acts_ref, token_ref, *refs):
    refs[-1][...] = contract_last(acts_ref[...], stack_rows(refs[:-1]))


def on_left(sketches, res_acts, token):
    rows, tokens = len(sketches) * sketches[0].shape[1], res_acts.shape[0]
    return pl.pallas_call(
        left_kernel,
        in_specs=[pl.BlockSpec(memory_space=pltpu.VMEM)] * (2 + len(sketches)),
        out_specs=pl.BlockSpec(memory_space=pltpu.VMEM),
        out_shape=jax.ShapeDtypeStruct((tokens, rows), F32),
        compiler_params=pltpu.CompilerParams(vmem_limit_bytes=VMEM_LIMIT),
        cost_estimate=cost(0, 0),
    )(res_acts, token, *sketches)


def sum_ranks(product, first, queries, rank):
    shape = (product.shape[1], queries)
    chosen = lax.broadcasted_iota(jnp.int32, shape, 0) // rank + first == lax.broadcasted_iota(jnp.int32, shape, 1)
    chosen = chosen.astype(F32).astype(BF16)
    total = 0.0
    for _ in range(3):
        term = product.astype(BF16)
        total = total + jnp.dot(term, chosen, preferred_element_type=F32)
        product = product - term.astype(F32)
    return total


def make_score_kernel(score_scale, wide, high):
    def score_kernel(place_ref, own_ref, other_ref, grads_ref, *refs):
        rights, out_ref = refs[:-1], refs[-1]
        queries = out_ref.shape[0]
        half, rank = queries // 2, rights[0].shape[1]
        place = place_ref[0]
        core, row, column = place % 2, place // 2 % high, place // (2 * high)
        chips = [(column + wide - x) % wide * high + (row + high - y) % high for x, y in STEPS]
        order = [2 * chip + core for chip in chips] + [2 * chip + 1 - core for chip in chips]
        total = 0.0
        for j, left_ref in enumerate((own_ref, other_ref)):
            right = jnp.concatenate([ref[i] for ref in rights for i in range(j, ref.shape[0], 2)], axis=0)
            product = left_ref[...] * contract_last(grads_ref[...], right)
            total = total + sum_ranks(product, j * half, queries, rank)
        sums = total.T * score_scale
        for i, query in enumerate(order):
            out_ref[pl.ds(query, 1), :] = sums[i : i + 1]

    return score_kernel


def all_scores(place, own, other, rights, res_grads, score_scale, sizes):
    queries = sum(x.shape[0] for x in rights)
    vmem = pl.BlockSpec(memory_space=pltpu.VMEM)
    return pl.pallas_call(
        make_score_kernel(score_scale, *sizes),
        in_specs=[pl.BlockSpec(memory_space=pltpu.SMEM)] + [vmem] * (3 + len(rights)),
        out_specs=vmem,
        out_shape=jax.ShapeDtypeStruct((queries, own.shape[0]), F32),
        compiler_params=pltpu.CompilerParams(vmem_limit_bytes=VMEM_LIMIT),
        cost_estimate=cost(2 * own.size * res_grads.shape[1], 2 * res_grads.size),
    )(place, own, other, res_grads, *rights)


def from_back(block, axis, step):
    size = lax.axis_size(axis)
    return lax.ppermute(block, axis, [(i, (i + step) % size) for i in range(size)])


STEPS = ((0, 0), (1, 0), (0, 1), (1, 1), (0, 3), (1, 3), (0, 2), (1, 2))


def local(query_acts, query_grads, sketch_maps, res_acts, res_grads):
    rank, outs = sketch_maps.shape[1:]
    groups = lax.axis_size(TOK)
    score_scale = 1.0 / math.sqrt(rank * outs * query_acts.shape[1] * groups)

    parts = exchange(partial_sketch(sketch_maps, query_grads, query_acts, groups), TOK)
    sketch = exchange(sum_pieces(parts), TOK)
    place = lax.axis_index(QUERY).astype(jnp.int32).reshape(1)
    sketch, place = lax.optimization_barrier((sketch, place))
    right_part, gram = partial_right(sketch, query_acts, query_grads)
    sketch, right_part = lax.optimization_barrier((sketch, right_part))
    right_parts = exchange(right_part, TOK)

    inverse = invert(gram)
    right = solve_right(right_parts, inverse)

    beside, behind, ahead = from_back(sketch, "xlo", 1), from_back(sketch, "y", 1), from_back(sketch, "y", 3)
    _, beside, behind = lax.optimization_barrier((inverse, beside, behind))
    corners = [from_back(beside, "y", 1), from_back(beside, "y", 3)]
    across = [from_back(behind, "y", 1), from_back(corners[1], "y", 3)]
    right, ahead = lax.optimization_barrier((right, ahead))
    both = jnp.stack([right, swap_cores(right)])
    early = [sketch, beside, behind, corners[0], ahead, corners[1], across[0]]
    both, acts, *early = lax.optimization_barrier((both, res_acts, *early))
    both = jnp.concatenate([both, from_back(both, "xlo", 1)])
    other_early = [swap_cores(block) for block in early[:4]]
    both, token, *later = lax.optimization_barrier((both, touch(acts), *early[4:]))
    other_early += [swap_cores(block) for block in later]
    rights = [both] + [from_back(both, "y", step) for step in (1, 3, 2)]
    token, last, *early = lax.optimization_barrier((token, across[1], *early))
    own_left = on_left(early + [last], acts, token)
    other_left = on_left(other_early + [swap_cores(last)], acts, token)
    sizes = lax.axis_size("xlo"), lax.axis_size("y")
    return all_scores(place, own_left, other_left, rights, res_grads, score_scale, sizes)


def solution(mesh):
    fine = Mesh(mesh.devices.reshape(2, 4, 2, 8, 2), QUERY + TOK)
    in_specs = (
        P(QUERY, TOK, None),
        P(QUERY, TOK, None),
        P(QUERY, None, None),
        P(QUERY + TOK, None),
        P(QUERY + TOK, None),
    )
    return jax.shard_map(local, mesh=fine, in_specs=in_specs, out_specs=P(None, QUERY + TOK), check_vma=False)
```

time: 116 us -> 93.1 us (0.80); the launches traced: 114 us -> 92.3 us
  blocking collectives: 38.2 us -> 23 us
  matrix products: 17.6 us -> 2.41 us
  starting transfers between devices: 9.57 us -> 23.4 us
  between operations: 13.5 us -> 0.13 us
  Pallas kernels: 0 us -> 12.9 us
  other arithmetic: 7.45 us -> 0.02 us
  waiting for transfers between devices: 23.3 us -> 26.4 us
    all_gather x1 -> x0, waiting for transfers between devices: 15.8 us -> none  [local(): lefts = lax.all_gather(sketch, QUERY, axis=0, tiled=True)]
    ppermute x0 -> x20, waiting for transfers between devices: none -> 15.4 us  [the longest x11 14.9 us: from_back(): lax.ppermute(block, axis, [(i, (i + step) % size) for i in range(size)])]
    all_to_all x2 -> x1, blocking collectives: 38.2 us -> 23 us  [exchange(): return lax.all_to_all(blocks, axes, 0, 0, tiled=True)]
    dot_general x7 -> x1, matrix products: 17.4 us -> 2.41 us  [partial_sketch(): jnp.dot(projected, query_acts[0], preferred_element_type=F32).astype(BF16)]
    ppermute x0 -> x20, starting transfers between devices: none -> 13.4 us  [the longest x11 11.4 us: from_back(): lax.ppermute(block, axis, [(i, (i + step) % size) for i in range(size)])]
    pallas_call x0 -> x8, Pallas kernels: none -> 12.9 us  [the longest x2 4.73 us: on_left(): pl.pallas_call(left_kernel, in_specs=[pl.BlockSpec(memory_space=pltpu.VME...]
    another operation x5 -> x1, other arithmetic: 6.69 us -> 0.01 us  [local(): both = jnp.stack([right, swap_cores(right)])]
    all_to_all x2, waiting for transfers between devices: 7.54 us -> 10.9 us  [exchange(): return lax.all_to_all(blocks, axes, 0, 0, tiled=True)]
  transfers between devices with their start and end apart: 3 -> 22, of which waited for: 2 -> 9; matrix products, arithmetic and copies ran while one was open for 19% -> 0% of each run, Pallas kernels for 0% -> 8%
where the time goes in v3:
time: 93.1 us; the launch traced here: 92.3 us
  waiting for transfers between devices  26.4 us (28%)
  starting transfers between devices  23.4 us (25%)
  blocking collectives  23 us (25%)
  Pallas kernels  12.9 us (14%)
  local copies, waits for them, and re-layouts  4.19 us (5%)
  matrix products  2.41 us (3%)
    all_to_all x1, blocking collectives, exchange(): return lax.all_to_all(blocks, axes, 0, 0, tiled=True)  23 us
    ppermute x11, waiting for transfers between devices, from_back(): lax.ppermute(block, axis, [(i, (i + step) % size) for i in range(size)])  14.9 us
    ppermute x11, starting transfers between devices, from_back(): lax.ppermute(block, axis, [(i, (i + step) % size) for i in range(size)])  11.4 us
    all_to_all x2, waiting for transfers between devices, exchange(): return lax.all_to_all(blocks, axes, 0, 0, tiled=True)  10.9 us
    all_to_all x2, starting transfers between devices, exchange(): return lax.all_to_all(blocks, axes, 0, 0, tiled=True)  9.99 us
    pallas_call x2, Pallas kernels, on_left(): pl.pallas_call(left_kernel, in_specs=[pl.BlockSpec(memory_space=pltpu.VME...  4.73 us
    unnamed x10, local copies, waits for them, and re-layouts  4.15 us
    pallas_call x1, Pallas kernels, invert(): pl.pallas_call(inverse_kernel, out_shape=jax.ShapeDtypeStruct(gram.shape,...  2.68 us
  transfers between devices with their start and end apart: 22, of which 9 were waited for; matrix products, arithmetic and copies ran while one was open for 0% of the time, Pallas kernels for 8%

profile of v3, /device:TPU:32, one launch (start us, length us, event | category | flops | bytes accessed | tf_op | source)
XLA Modules:
  0.0 92.3 jit_solution(2015867515950704594)
XLA Ops:
  0.0 0.7 copy-done
  0.8 2.4 %convolution_convert_fusion = bf16[32,4096]{1,0:T(8,128)(2,1)S(1)} fusion(bf16[1,256,4096]{2,1,0:T(8,128)(2,1)} %acts_ref.1, bf16[1,256,512]{2,1,0:T(8,128)(2,1)} %grads_ref.2, bf16[1,32,512]{2,1,0:T(8,128)(2,1)S(1)} %copy-done), kind=kOutput, calls=%fused_computation | convolution fusion | flops 75636736 | bytes 2654208 | tf_op jit(solution)/shard_map/dot_general | solution.py:42
  3.2 23.0 %all_to_all.15.parts_ref = bf16[16,32,256]{2,1,0:T(8,128)(2,1)S(1)} all-to-all(bf16[16,32,256]{2,1,0:T(8,128)(2,1)S(1)} %bitcast.22), channel_id=1, replica_groups=mesh['xlo'=2,'y'=4,'core'=2,'z'=8,'xhi'=2] {'z','xhi'}, dimensions={0} | all-to-all | bytes 524288 | tf_op jit(solution)/shard_map/all_to_all | solution.py:28
  26.2 0.8 shard_map.55
  26.9 4.9 %all-to-all-start.1 = ((bf16[16,32,256]{2,1,0:T(8,128)(2,1)}), bf16[16,32,256]{2,1,0:T(8,128)(2,1)S(1)}, u32[]{:S(2)}, u32[]{:S(2)}) async-start(bf16[16,32,256]{2,1,0:T(8,128)(2,1)} %shard_map.55), calls=%async_computation.1 | async-start | bytes 524288 | tf_op jit(solution)/shard_map/all_to_all | solution.py:28
  31.8 10.8 %all-to-all-done.1.sketch_ref.refs_0_ = bf16[16,32,256]{2,1,0:T(8,128)(2,1)S(1)} async-done(((bf16[16,32,256]{2,1,0:T(8,128)(2,1)}), bf16[16,32,256]{2,1,0:T(8,128)(2,1)S(1)}, u32[]{:S(2)}, u32[]{:S(2)}) %all-to-all-start.1) | async-done | bytes 262176 | tf_op jit(solution)/shard_map/all_to_all | solution.py:28
  42.5 1.8 %shard_map.56 = (bf16[16,32,512]{2,1,0:T(8,128)(2,1)}, f32[32,32]{1,0:T(8,128)S(1)}) custom-call(bf16[16,32,256]{2,1,0:T(8,128)(2,1)S(1)} %all-to-all-done.1.sketch_ref.refs_0_, bf16[1,256,4096]{2,1,0:T(8,128)(2,1)S(1)} %copy-done.2, bf16[1,256,512]{2,1,0:T(8,128)(2,1)S(1)} %copy-done.4), custom_call_target="tpu_custom_call" | custom-call | flops 75497472 | bytes 2097152 | tf_op jit(solution)/shard_map/pallas_call | solution.py:72
  44.4 5.1 %all-to-all-start.2 = ((bf16[16,32,512]{2,1,0:T(8,128)(2,1)}), bf16[16,32,512]{2,1,0:T(8,128)(2,1)S(1)}, u32[]{:S(2)}, u32[]{:S(2)}) async-start(bf16[16,32,512]{2,1,0:T(8,128)(2,1)} %get-tuple-element.41), calls=%async_computation.2 | async-start | bytes 1048576 | tf_op jit(solution)/shard_map/all_to_all | solution.py:28
  49.5 3.1 %collective-permute-start = (bf16[16,32,256]{2,1,0:T(8,128)(2,1)S(1)}, bf16[16,32,256]{2,1,0:T(8,128)(2,1)S(1)}, u32[]{:S(2)}, u32[]{:S(2)}) collective-permute-start(bf16[16,32,256]{2,1,0:T(8,128)(2,1)S(1)} %all-to-all-done.1.sketch_ref.refs_0_), channel_id=1, source_target_pairs={{0,96},{32,0},{64,32},{96,64},{1,97},{33,1},{65,33},{97,65},{2,98}... | collective-permute-start | bytes 786440 | tf_op jit(solution)/shard_map/ppermute | solution.py:200
  52.6 0.6 collective-permute-start.2
  53.2 2.7 %shard_map.57.inverse_ref = f32[32,32]{1,0:T(8,128)S(1)} custom-call(f32[32,32]{1,0:T(8,128)S(1)} %get-tuple-element.42.gram_ref), custom_call_target="tpu_custom_call" | custom-call | flops 4294967296 | bytes 4194304 | tf_op jit(solution)/shard_map/pallas_call | solution.py:98
  55.8 6.0 %collective-permute-done.2.refs_1_ = bf16[16,32,256]{2,1,0:T(8,128)(2,1)S(1)} collective-permute-done((bf16[16,32,256]{2,1,0:T(8,128)(2,1)S(1)}, bf16[16,32,256]{2,1,0:T(8,128)(2,1)S(1)}, u32[]{:S(2)}, u32[]{:S(2)}) %collective-permute-start.2) | collective-permute-done | bytes 262176 | tf_op jit(solution)/shard_map/ppermute | solution.py:200
  61.8 0.7 collective-permute-start.5
  62.6 1.3 %collective-permute-start.4 = (bf16[16,32,256]{2,1,0:T(8,128)(2,1)S(1)}, bf16[16,32,256]{2,1,0:T(8,128)(2,1)S(1)}, u32[]{:S(2)}, u32[]{:S(2)}) collective-permute-start(bf16[16,32,256]{2,1,0:T(8,128)(2,1)S(1)} %collective-permute-done.2.refs_1_), channel_id=1, source_target_pairs={{0,32},{32,64},{64,96},{96,0},{1,33},{33,65},{65,97},{97,1},{2,34}... | collective-permute-start | bytes 786440 | tf_op jit(solution)/shard_map/ppermute | solution.py:200
  64.1 0.3 shard_map.58
  64.5 4.4 %collective-permute-done.5.refs_5_ = bf16[16,32,256]{2,1,0:T(8,128)(2,1)S(1)} collective-permute-done((bf16[16,32,256]{2,1,0:T(8,128)(2,1)S(1)}, bf16[16,32,256]{2,1,0:T(8,128)(2,1)S(1)}, u32[]{:S(2)}, u32[]{:S(2)}) %collective-permute-start.5) | collective-permute-done | bytes 262176 | tf_op jit(solution)/shard_map/ppermute | solution.py:200
  68.8 1.3 %collective-permute-start.8 = (bf16[16,32,256]{2,1,0:T(8,128)(2,1)S(1)}, bf16[16,32,256]{2,1,0:T(8,128)(2,1)S(1)}, u32[]{:S(2)}, u32[]{:S(2)}) collective-permute-start(bf16[16,32,256]{2,1,0:T(8,128)(2,1)S(1)} %collective-permute-done.5.refs_5_), channel_id=1, source_target_pairs={{0,96},{32,0},{64,32},{96,64},{1,97},{33,1},{65,33},{97,65},{2,98}... | collective-permute-start | bytes 786440 | tf_op jit(solution)/shard_map/ppermute | solution.py:200
  70.2 2.8 %collective-permute-done.6.refs_6_ = bf16[16,32,256]{2,1,0:T(8,128)(2,1)S(1)} collective-permute-done((bf16[16,32,256]{2,1,0:T(8,128)(2,1)S(1)}, bf16[16,32,256]{2,1,0:T(8,128)(2,1)S(1)}, u32[]{:S(2)}, u32[]{:S(2)}) %collective-permute-start.6) | collective-permute-done | bytes 262176 | tf_op jit(solution)/shard_map/ppermute | solution.py:200
  73.0 1.5 %collective-permute-start.7 = (bf16[2,32,512]{2,1,0:T(8,128)(2,1)S(1)}, bf16[2,32,512]{2,1,0:T(8,128)(2,1)S(1)}, u32[]{:S(2)}, u32[]{:S(2)}) collective-permute-start(bf16[2,32,512]{2,1,0:T(8,128)(2,1)S(1)} %pad_maximum_fusion.1), channel_id=1, source_target_pairs={{0,128},{128,0},{1,129},{129,1},{2,130},{130,2},{3,131},{131,3},{4... | collective-permute-start | bytes 196616 | tf_op jit(solution)/shard_map/ppermute | solution.py:200
  74.6 0.3 collective-permute-start.11
  74.9 3.4 %copy-done.1 = bf16[1024,4096]{1,0:T(8,128)(2,1)S(1)} copy-done((bf16[1024,4096]{1,0:T(8,128)(2,1)S(1)}, bf16[1024,4096]{1,0:T(8,128)(2,1)}, u32[]{:S(2)}) %copy-start.1) | copy-done | bytes 8388632
  78.6 0.4 collective-permute-start.13
  78.9 0.2 collective-permute-start.14
  79.2 0.3 collective-permute-start.15
  79.5 0.3 collective-permute-start.16
  79.8 0.4 collective-permute-done.13.refs_4_
  80.2 2.9 %collective-permute-start.18 = (bf16[4,32,512]{2,1,0:T(8,128)(2,1)S(1)}, bf16[4,32,512]{2,1,0:T(8,128)(2,1)S(1)}, u32[]{:S(2)}, u32[]{:S(2)}) collective-permute-start(bf16[4,32,512]{2,1,0:T(8,128)(2,1)S(1)} %pad_maximum_fusion.refs_0_), channel_id=1, source_target_pairs={{0,96},{32,0},{64,32},{96,64},{1,97},{33,1},{65,33},{97,65},{2,98}... | collective-permute-start | bytes 393224 | tf_op jit(solution)/shard_map/ppermute | solution.py:200
  83.1 2.4 %shard_map.60.own_ref = f32[1024,256]{1,0:T(8,128)S(1)} custom-call(bf16[1024,4096]{1,0:T(8,128)(2,1)S(1)} %copy-done.1, bf16[16,128]{1,0:T(8,128)(2,1)S(1)} %shard_map.59.token_ref, bf16[16,32,256]{2,1,0:T(8,128)(2,1)S(1)} %all-to-all-done.1.sketch_ref.refs_0_, bf16[16,32,256]{2,1,0:T(8,128)(2,1)S(1)} %collective-permute-done.2.refs_1_, ...), custom_call_target="tpu_custom_call" | custom-call | tf_op jit(solution)/shard_map/pallas_call | solution.py:142
  85.5 2.4 %shard_map.61.other_ref = f32[1024,256]{1,0:T(8,128)S(1)} custom-call(bf16[1024,4096]{1,0:T(8,128)(2,1)S(1)} %copy-done.1, bf16[16,128]{1,0:T(8,128)(2,1)S(1)} %shard_map.59.token_ref, bf16[16,32,256]{2,1,0:T(8,128)(2,1)S(1)} %collective-permute-done.9.refs_0_, bf16[16,32,256]{2,1,0:T(8,128)(2,1)S(1)} %collective-permute-done.10.refs_1_, ...), custom_call_target="tpu_custom_call" | custom-call | tf_op jit(solution)/shard_map/pallas_call | solution.py:142
  87.9 0.9 collective-permute-done.18.refs_2_
  88.8 0.9 collective-permute-done.19.refs_3_
  89.7 2.7 %shard_map.62 = f32[16,1024]{1,0:T(8,128)} custom-call(s32[1]{0:T(128)} %bitcast.4.place_ref, f32[1024,256]{1,0:T(8,128)S(1)} %shard_map.60.own_ref, f32[1024,256]{1,0:T(8,128)S(1)} %shard_map.61.other_ref, bf16[1024,512]{1,0:T(8,128)(2,1)S(1)} %copy-done.3, bf16[4,32,512]{2,1,0:T(8,128)(2,1)S(1)} %pad_maximum_fusion.refs_0_, ...), custom_call_target="tpu_custom_call" | custom-call | flops 268435456 | bytes 1048576 | tf_op jit(solution)/shard_map/pallas_call | solution.py:188
  (35 shorter events, 1.0 us)
Async XLA Ops:
  0.0 0.8 copy-start
  0.0 42.5 %copy-start.2 = (bf16[1,256,4096]{2,1,0:T(8,128)(2,1)S(1)}, bf16[1,256,4096]{2,1,0:T(8,128)(2,1)}, u32[]{:S(2)}) copy-start(bf16[1,256,4096]{2,1,0:T(8,128)(2,1)} %acts_ref.1) | copy-start | bytes 6291460
  0.0 42.5 %copy-start.4 = (bf16[1,256,512]{2,1,0:T(8,128)(2,1)S(1)}, bf16[1,256,512]{2,1,0:T(8,128)(2,1)}, u32[]{:S(2)}) copy-start(bf16[1,256,512]{2,1,0:T(8,128)(2,1)} %grads_ref.2) | copy-start | bytes 786436
  26.9 15.6 %all-to-all-start.1 = ((bf16[16,32,256]{2,1,0:T(8,128)(2,1)}), bf16[16,32,256]{2,1,0:T(8,128)(2,1)S(1)}, u32[]{:S(2)}, u32[]{:S(2)}) async-start(bf16[16,32,256]{2,1,0:T(8,128)(2,1)} %shard_map.55), calls=%async_computation.1 | async-start | bytes 524288 | tf_op jit(solution)/shard_map/all_to_all | solution.py:28
  44.4 19.7 %all-to-all-start.2 = ((bf16[16,32,512]{2,1,0:T(8,128)(2,1)}), bf16[16,32,512]{2,1,0:T(8,128)(2,1)S(1)}, u32[]{:S(2)}, u32[]{:S(2)}) async-start(bf16[16,32,512]{2,1,0:T(8,128)(2,1)} %get-tuple-element.41), calls=%async_computation.2 | async-start | bytes 1048576 | tf_op jit(solution)/shard_map/all_to_all | solution.py:28
  49.5 14.9 %collective-permute-start = (bf16[16,32,256]{2,1,0:T(8,128)(2,1)S(1)}, bf16[16,32,256]{2,1,0:T(8,128)(2,1)S(1)}, u32[]{:S(2)}, u32[]{:S(2)}) collective-permute-start(bf16[16,32,256]{2,1,0:T(8,128)(2,1)S(1)} %all-to-all-done.1.sketch_ref.refs_0_), channel_id=1, source_target_pairs={{0,96},{32,0},{64,32},{96,64},{1,97},{33,1},{65,33},{97,65},{2,98}... | collective-permute-start | bytes 786440 | tf_op jit(solution)/shard_map/ppermute | solution.py:200
  52.6 9.3 %collective-permute-start.2 = (bf16[16,32,256]{2,1,0:T(8,128)(2,1)S(1)}, bf16[16,32,256]{2,1,0:T(8,128)(2,1)S(1)}, u32[]{:S(2)}, u32[]{:S(2)}) collective-permute-start(bf16[16,32,256]{2,1,0:T(8,128)(2,1)S(1)} %all-to-all-done.1.sketch_ref.refs_0_), channel_id=1, source_target_pairs={{0,128},{128,0},{1,129},{129,1},{2,130},{130,2},{3,131},{131,3},{4... | collective-permute-start | bytes 786440 | tf_op jit(solution)/shard_map/ppermute | solution.py:200
  53.2 8.7 %collective-permute-start.3 = (bf16[16,32,256]{2,1,0:T(8,128)(2,1)S(1)}, bf16[16,32,256]{2,1,0:T(8,128)(2,1)S(1)}, u32[]{:S(2)}, u32[]{:S(2)}) collective-permute-start(bf16[16,32,256]{2,1,0:T(8,128)(2,1)S(1)} %all-to-all-done.1.sketch_ref.refs_0_), channel_id=1, source_target_pairs={{0,32},{32,64},{64,96},{96,0},{1,33},{33,65},{65,97},{97,1},{2,34}... | collective-permute-start | bytes 786440 | tf_op jit(solution)/shard_map/ppermute | solution.py:200
  61.8 7.0 %collective-permute-start.5 = (bf16[16,32,256]{2,1,0:T(8,128)(2,1)S(1)}, bf16[16,32,256]{2,1,0:T(8,128)(2,1)S(1)}, u32[]{:S(2)}, u32[]{:S(2)}) collective-permute-start(bf16[16,32,256]{2,1,0:T(8,128)(2,1)S(1)} %collective-permute-done.2.refs_1_), channel_id=1, source_target_pairs={{0,96},{32,0},{64,32},{96,64},{1,97},{33,1},{65,33},{97,65},{2,98}... | collective-permute-start | bytes 786440 | tf_op jit(solution)/shard_map/ppermute | solution.py:200
  62.6 7.6 %collective-permute-start.4 = (bf16[16,32,256]{2,1,0:T(8,128)(2,1)S(1)}, bf16[16,32,256]{2,1,0:T(8,128)(2,1)S(1)}, u32[]{:S(2)}, u32[]{:S(2)}) collective-permute-start(bf16[16,32,256]{2,1,0:T(8,128)(2,1)S(1)} %collective-permute-done.2.refs_1_), channel_id=1, source_target_pairs={{0,32},{32,64},{64,96},{96,0},{1,33},{33,65},{65,97},{97,1},{2,34}... | collective-permute-start | bytes 786440 | tf_op jit(solution)/shard_map/ppermute | solution.py:200
  63.9 9.1 %collective-permute-start.6 = (bf16[16,32,256]{2,1,0:T(8,128)(2,1)S(1)}, bf16[16,32,256]{2,1,0:T(8,128)(2,1)S(1)}, u32[]{:S(2)}, u32[]{:S(2)}) collective-permute-start(bf16[16,32,256]{2,1,0:T(8,128)(2,1)S(1)} %collective-permute-done.3.refs_2_), channel_id=1, source_target_pairs={{0,32},{32,64},{64,96},{96,0},{1,33},{33,65},{65,97},{97,1},{2,34}... | collective-permute-start | bytes 786440 | tf_op jit(solution)/shard_map/ppermute | solution.py:200
  64.4 5.8 %collective-permute-start.1 = (bf16[32,512]{1,0:T(8,128)(2,1)S(1)}, bf16[32,512]{1,0:T(8,128)(2,1)S(1)}, u32[]{:S(2)}, u32[]{:S(2)}) collective-permute-start(bf16[32,512]{1,0:T(8,128)(2,1)S(1)} %shard_map.58), channel_id=1, source_target_pairs={{0,16},{16,0},{1,17},{17,1},{2,18},{18,2},{3,19},{19,3},{4,20},{20... | collective-permute-start | bytes 98312 | tf_op jit(solution)/shard_map/ppermute | solution.py:32
  68.8 9.7 %collective-permute-start.8 = (bf16[16,32,256]{2,1,0:T(8,128)(2,1)S(1)}, bf16[16,32,256]{2,1,0:T(8,128)(2,1)S(1)}, u32[]{:S(2)}, u32[]{:S(2)}) collective-permute-start(bf16[16,32,256]{2,1,0:T(8,128)(2,1)S(1)} %collective-permute-done.5.refs_5_), channel_id=1, source_target_pairs={{0,96},{32,0},{64,32},{96,64},{1,97},{33,1},{65,33},{97,65},{2,98}... | collective-permute-start | bytes 786440 | tf_op jit(solution)/shard_map/ppermute | solution.py:200
  73.0 6.0 %collective-permute-start.9 = (bf16[16,32,256]{2,1,0:T(8,128)(2,1)S(1)}, bf16[16,32,256]{2,1,0:T(8,128)(2,1)S(1)}, u32[]{:S(2)}, u32[]{:S(2)}) collective-permute-start(bf16[16,32,256]{2,1,0:T(8,128)(2,1)S(1)} %all-to-all-done.1.sketch_ref.refs_0_), channel_id=1, source_target_pairs={{0,16},{16,0},{1,17},{17,1},{2,18},{18,2},{3,19},{19,3},{4,20},{20... | collective-permute-start | bytes 786440 | tf_op jit(solution)/shard_map/ppermute | solution.py:32
  73.0 5.3 %collective-permute-start.7 = (bf16[2,32,512]{2,1,0:T(8,128)(2,1)S(1)}, bf16[2,32,512]{2,1,0:T(8,128)(2,1)S(1)}, u32[]{:S(2)}, u32[]{:S(2)}) collective-permute-start(bf16[2,32,512]{2,1,0:T(8,128)(2,1)S(1)} %pad_maximum_fusion.1), channel_id=1, source_target_pairs={{0,128},{128,0},{1,129},{129,1},{2,130},{130,2},{3,131},{131,3},{4... | collective-permute-start | bytes 196616 | tf_op jit(solution)/shard_map/ppermute | solution.py:200
  74.4 4.8 %collective-permute-start.10 = (bf16[16,32,256]{2,1,0:T(8,128)(2,1)S(1)}, bf16[16,32,256]{2,1,0:T(8,128)(2,1)S(1)}, u32[]{:S(2)}, u32[]{:S(2)}) collective-permute-start(bf16[16,32,256]{2,1,0:T(8,128)(2,1)S(1)} %collective-permute-done.2.refs_1_), channel_id=1, source_target_pairs={{0,16},{16,0},{1,17},{17,1},{2,18},{18,2},{3,19},{19,3},{4,20},{20... | collective-permute-start | bytes 786440 | tf_op jit(solution)/shard_map/ppermute | solution.py:32
  74.6 4.8 %collective-permute-start.11 = (bf16[16,32,256]{2,1,0:T(8,128)(2,1)S(1)}, bf16[16,32,256]{2,1,0:T(8,128)(2,1)S(1)}, u32[]{:S(2)}, u32[]{:S(2)}) collective-permute-start(bf16[16,32,256]{2,1,0:T(8,128)(2,1)S(1)} %collective-permute-done.3.refs_2_), channel_id=1, source_target_pairs={{0,16},{16,0},{1,17},{17,1},{2,18},{18,2},{3,19},{19,3},{4,20},{20... | collective-permute-start | bytes 786440 | tf_op jit(solution)/shard_map/ppermute | solution.py:32
  74.9 3.4 %copy-start.1 = (bf16[1024,4096]{1,0:T(8,128)(2,1)S(1)}, bf16[1024,4096]{1,0:T(8,128)(2,1)}, u32[]{:S(2)}) copy-start(bf16[1024,4096]{1,0:T(8,128)(2,1)} %acts_ref.4) | copy-start | bytes 25165828
  78.3 1.5 %collective-permute-start.12 = (bf16[16,32,256]{2,1,0:T(8,128)(2,1)S(1)}, bf16[16,32,256]{2,1,0:T(8,128)(2,1)S(1)}, u32[]{:S(2)}, u32[]{:S(2)}) collective-permute-start(bf16[16,32,256]{2,1,0:T(8,128)(2,1)S(1)} %collective-permute-done.4.refs_3_), channel_id=1, source_target_pairs={{0,16},{16,0},{1,17},{17,1},{2,18},{18,2},{3,19},{19,3},{4,20},{20... | collective-permute-start | bytes 786440 | tf_op jit(solution)/shard_map/ppermute | solution.py:32
  78.6 1.7 %collective-permute-start.13 = (bf16[16,32,256]{2,1,0:T(8,128)(2,1)S(1)}, bf16[16,32,256]{2,1,0:T(8,128)(2,1)S(1)}, u32[]{:S(2)}, u32[]{:S(2)}) collective-permute-start(bf16[16,32,256]{2,1,0:T(8,128)(2,1)S(1)} %collective-permute-done.refs_4_), channel_id=1, source_target_pairs={{0,16},{16,0},{1,17},{17,1},{2,18},{18,2},{3,19},{19,3},{4,20},{20... | collective-permute-start | bytes 786440 | tf_op jit(solution)/shard_map/ppermute | solution.py:32
  78.9 4.2 %collective-permute-start.14 = (bf16[16,32,256]{2,1,0:T(8,128)(2,1)S(1)}, bf16[16,32,256]{2,1,0:T(8,128)(2,1)S(1)}, u32[]{:S(2)}, u32[]{:S(2)}) collective-permute-start(bf16[16,32,256]{2,1,0:T(8,128)(2,1)S(1)} %collective-permute-done.5.refs_5_), channel_id=1, source_target_pairs={{0,16},{16,0},{1,17},{17,1},{2,18},{18,2},{3,19},{19,3},{4,20},{20... | collective-permute-start | bytes 786440 | tf_op jit(solution)/shard_map/ppermute | solution.py:32
  79.2 6.3 %collective-permute-start.15 = (bf16[16,32,256]{2,1,0:T(8,128)(2,1)S(1)}, bf16[16,32,256]{2,1,0:T(8,128)(2,1)S(1)}, u32[]{:S(2)}, u32[]{:S(2)}) collective-permute-start(bf16[16,32,256]{2,1,0:T(8,128)(2,1)S(1)} %collective-permute-done.6.refs_6_), channel_id=1, source_target_pairs={{0,16},{16,0},{1,17},{17,1},{2,18},{18,2},{3,19},{19,3},{4,20},{20... | collective-permute-start | bytes 786440 | tf_op jit(solution)/shard_map/ppermute | solution.py:32
  79.5 6.0 %collective-permute-start.16 = (bf16[16,32,256]{2,1,0:T(8,128)(2,1)S(1)}, bf16[16,32,256]{2,1,0:T(8,128)(2,1)S(1)}, u32[]{:S(2)}, u32[]{:S(2)}) collective-permute-start(bf16[16,32,256]{2,1,0:T(8,128)(2,1)S(1)} %collective-permute-done.8.refs_7_), channel_id=1, source_target_pairs={{0,16},{16,0},{1,17},{17,1},{2,18},{18,2},{3,19},{19,3},{4,20},{20... | collective-permute-start | bytes 786440 | tf_op jit(solution)/shard_map/ppermute | solution.py:32
  79.8 8.0 %collective-permute-start.17 = (bf16[4,32,512]{2,1,0:T(8,128)(2,1)S(1)}, bf16[4,32,512]{2,1,0:T(8,128)(2,1)S(1)}, u32[]{:S(2)}, u32[]{:S(2)}) collective-permute-start(bf16[4,32,512]{2,1,0:T(8,128)(2,1)S(1)} %pad_maximum_fusion.refs_0_), channel_id=1, source_target_pairs={{0,32},{32,64},{64,96},{96,0},{1,33},{33,65},{65,97},{97,1},{2,34}... | collective-permute-start | bytes 393224 | tf_op jit(solution)/shard_map/ppermute | solution.py:200
  80.2 8.6 %collective-permute-start.18 = (bf16[4,32,512]{2,1,0:T(8,128)(2,1)S(1)}, bf16[4,32,512]{2,1,0:T(8,128)(2,1)S(1)}, u32[]{:S(2)}, u32[]{:S(2)}) collective-permute-start(bf16[4,32,512]{2,1,0:T(8,128)(2,1)S(1)} %pad_maximum_fusion.refs_0_), channel_id=1, source_target_pairs={{0,96},{32,0},{64,32},{96,64},{1,97},{33,1},{65,33},{97,65},{2,98}... | collective-permute-start | bytes 393224 | tf_op jit(solution)/shard_map/ppermute | solution.py:200
  83.1 6.6 %collective-permute-start.19 = (bf16[4,32,512]{2,1,0:T(8,128)(2,1)S(1)}, bf16[4,32,512]{2,1,0:T(8,128)(2,1)S(1)}, u32[]{:S(2)}, u32[]{:S(2)}) collective-permute-start(bf16[4,32,512]{2,1,0:T(8,128)(2,1)S(1)} %pad_maximum_fusion.refs_0_), channel_id=1, source_target_pairs={{0,64},{32,96},{64,0},{96,32},{1,65},{33,97},{65,1},{97,33},{2,66}... | collective-permute-start | bytes 393224 | tf_op jit(solution)/shard_map/ppermute | solution.py:200
  85.5 4.2 %copy-start.3 = (bf16[1024,512]{1,0:T(8,128)(2,1)S(1)}, bf16[1024,512]{1,0:T(8,128)(2,1)}, u32[]{:S(2)}) copy-start(bf16[1024,512]{1,0:T(8,128)(2,1)} %grads_ref.3) | copy-start | bytes 3145732

commit v4 on v3

--- a/solution.py
+++ b/solution.py
@@ -154,7 +154,7 @@
     chosen = lax.broadcasted_iota(jnp.int32, shape, 0) // rank + first == lax.broadcasted_iota(jnp.int32, shape, 1)
     chosen = chosen.astype(F32).astype(BF16)
     total = 0.0
-    for _ in range(3):
+    for _ in range(2):
         term = product.astype(BF16)
         total = total + jnp.dot(term, chosen, preferred_element_type=F32)
         product = product - term.astype(F32)
@@ -208,10 +208,11 @@
     groups = lax.axis_size(TOK)
     score_scale = 1.0 / math.sqrt(rank * outs * query_acts.shape[1] * groups)
 
-    parts = exchange(partial_sketch(sketch_maps, query_grads, query_acts, groups), TOK)
+    place = lax.axis_index(QUERY).astype(jnp.int32).reshape(1)
+    partial = partial_sketch(sketch_maps, query_grads, query_acts, groups)
+    partial, place = lax.optimization_barrier((partial, place))
+    parts = exchange(partial, TOK)
     sketch = exchange(sum_pieces(parts), TOK)
-    place = lax.axis_index(QUERY).astype(jnp.int32).reshape(1)
-    sketch, place = lax.optimization_barrier((sketch, place))
     right_part, gram = partial_right(sketch, query_acts, query_grads)
     sketch, right_part = lax.optimization_barrier((sketch, right_part))
     right_parts = exchange(right_part, TOK)

time: 93.1 us -> 91.7 us (0.985)
  blocking collectives: 23 us -> 38.1 us
  waiting for transfers between devices: 26.4 us -> 17.8 us
  starting transfers between devices: 23.4 us -> 16.4 us
  Pallas kernels: 12.9 us -> 11.9 us
    all_to_all x1 -> x2, blocking collectives: 23 us -> 38.1 us  [exchange(): return lax.all_to_all(blocks, axes, 0, 0, tiled=True)]
    all_to_all x2 -> x1, waiting for transfers between devices: 10.9 us -> 0.01 us  [exchange(): return lax.all_to_all(blocks, axes, 0, 0, tiled=True)]
    all_to_all x2 -> x1, starting transfers between devices: 9.99 us -> 5 us  [exchange(): return lax.all_to_all(blocks, axes, 0, 0, tiled=True)]
    ppermute x11, waiting for transfers between devices: 14.9 us -> 17.6 us  [from_back(): lax.ppermute(block, axis, [(i, (i + step) % size) for i in range(size)])]
    ppermute x11, starting transfers between devices: 11.4 us -> 9.38 us  [from_back(): lax.ppermute(block, axis, [(i, (i + step) % size) for i in range(size)])]
  transfers between devices with their start and end apart: 22 -> 21, of which waited for: 9 -> 8; matrix products, arithmetic and copies ran while one was open for 0% -> 0% of each run, Pallas kernels for 8% -> 8%
where the time goes in v4:
time: 91.7 us; the launch traced here: 91.1 us
  blocking collectives  38.1 us (42%)
  waiting for transfers between devices  17.8 us (19%)
  starting transfers between devices  16.4 us (18%)
  Pallas kernels  11.9 us (13%)
  local copies, waits for them, and re-layouts  4.19 us (5%)
  matrix products  2.54 us (3%)
    all_to_all x2, blocking collectives, exchange(): return lax.all_to_all(blocks, axes, 0, 0, tiled=True)  38.1 us
    ppermute x11, waiting for transfers between devices, from_back(): lax.ppermute(block, axis, [(i, (i + step) % size) for i in range(size)])  17.6 us
    ppermute x11, starting transfers between devices, from_back(): lax.ppermute(block, axis, [(i, (i + step) % size) for i in range(size)])  9.38 us
    all_to_all x1, starting transfers between devices, exchange(): return lax.all_to_all(blocks, axes, 0, 0, tiled=True)  5 us
    pallas_call x2, Pallas kernels, on_left(): pl.pallas_call(left_kernel, in_specs=[pl.BlockSpec(memory_space=pltpu.VME...  4.73 us
    unnamed x10, local copies, waits for them, and re-layouts  4.15 us
    pallas_call x1, Pallas kernels, invert(): pl.pallas_call(inverse_kernel, out_shape=jax.ShapeDtypeStruct(gram.shape,...  2.68 us
    dot_general x1, matrix products, partial_sketch(): jnp.dot(projected, query_acts[0], preferred_element_type=F32).astype(BF16)  2.54 us
  transfers between devices with their start and end apart: 21, of which 8 were waited for; matrix products, arithmetic and copies ran while one was open for 0% of the time, Pallas kernels for 8%

profile of v4, /device:TPU:32, one launch (start us, length us, event | category | flops | bytes accessed | tf_op | source)
XLA Modules:
  0.0 91.1 jit_solution(14418337088895484068)
XLA Ops:
  0.0 0.8 copy-done
  0.8 2.5 %convolution_convert_fusion = bf16[32,4096]{1,0:T(8,128)(2,1)S(1)} fusion(bf16[1,256,4096]{2,1,0:T(8,128)(2,1)} %acts_ref.1, bf16[1,256,512]{2,1,0:T(8,128)(2,1)} %grads_ref.2, bf16[1,32,512]{2,1,0:T(8,128)(2,1)S(1)} %copy-done), kind=kOutput, calls=%fused_computation | convolution fusion | flops 75636736 | bytes 2654208 | tf_op jit(solution)/shard_map/dot_general | solution.py:42
  3.4 23.0 %all_to_all.15.parts_ref = bf16[16,32,256]{2,1,0:T(8,128)(2,1)S(1)} all-to-all(bf16[16,32,256]{2,1,0:T(8,128)(2,1)S(1)} %bitcast.22), channel_id=1, replica_groups=mesh['xlo'=2,'y'=4,'core'=2,'z'=8,'xhi'=2] {'z','xhi'}, dimensions={0} | all-to-all | bytes 524288 | tf_op jit(solution)/shard_map/all_to_all | solution.py:28
  26.4 15.1 %all_to_all.16.sketch_ref.refs_0_ = bf16[16,32,256]{2,1,0:T(8,128)(2,1)S(1)} all-to-all(bf16[16,32,256]{2,1,0:T(8,128)(2,1)S(1)} %shard_map.55), channel_id=1, replica_groups=mesh['xlo'=2,'y'=4,'core'=2,'z'=8,'xhi'=2] {'z','xhi'}, dimensions={0} | all-to-all | bytes 524288 | tf_op jit(solution)/shard_map/all_to_all | solution.py:28
  41.5 1.8 %shard_map.56 = (bf16[16,32,512]{2,1,0:T(8,128)(2,1)}, f32[32,32]{1,0:T(8,128)S(1)}) custom-call(bf16[16,32,256]{2,1,0:T(8,128)(2,1)S(1)} %all_to_all.16.sketch_ref.refs_0_, bf16[1,256,4096]{2,1,0:T(8,128)(2,1)S(1)} %copy-done.2, bf16[1,256,512]{2,1,0:T(8,128)(2,1)S(1)} %copy-done.4), custom_call_target="tpu_custom_call" | custom-call | flops 75497472 | bytes 2097152 | tf_op jit(solution)/shard_map/pallas_call | solution.py:72
  43.3 5.0 %all-to-all-start.2 = ((bf16[16,32,512]{2,1,0:T(8,128)(2,1)}), bf16[16,32,512]{2,1,0:T(8,128)(2,1)S(1)}, u32[]{:S(2)}, u32[]{:S(2)}) async-start(bf16[16,32,512]{2,1,0:T(8,128)(2,1)} %get-tuple-element.41), calls=%async_computation.2 | async-start | bytes 1048576 | tf_op jit(solution)/shard_map/all_to_all | solution.py:28
  48.3 3.0 %collective-permute-start = (bf16[16,32,256]{2,1,0:T(8,128)(2,1)S(1)}, bf16[16,32,256]{2,1,0:T(8,128)(2,1)S(1)}, u32[]{:S(2)}, u32[]{:S(2)}) collective-permute-start(bf16[16,32,256]{2,1,0:T(8,128)(2,1)S(1)} %all_to_all.16.sketch_ref.refs_0_), channel_id=1, source_target_pairs={{0,96},{32,0},{64,32},{96,64},{1,97},{33,1},{65,33},{97,65},{2,98}... | collective-permute-start | bytes 786440 | tf_op jit(solution)/shard_map/ppermute | solution.py:200
  51.4 0.6 collective-permute-start.2
  51.9 2.7 %shard_map.57.inverse_ref = f32[32,32]{1,0:T(8,128)S(1)} custom-call(f32[32,32]{1,0:T(8,128)S(1)} %get-tuple-element.42.gram_ref), custom_call_target="tpu_custom_call" | custom-call | flops 4294967296 | bytes 4194304 | tf_op jit(solution)/shard_map/pallas_call | solution.py:98
  54.6 6.4 %collective-permute-done.2.refs_1_ = bf16[16,32,256]{2,1,0:T(8,128)(2,1)S(1)} collective-permute-done((bf16[16,32,256]{2,1,0:T(8,128)(2,1)S(1)}, bf16[16,32,256]{2,1,0:T(8,128)(2,1)S(1)}, u32[]{:S(2)}, u32[]{:S(2)}) %collective-permute-start.2) | collective-permute-done | bytes 262176 | tf_op jit(solution)/shard_map/ppermute | solution.py:200
  61.1 2.0 %collective-permute-start.4 = (bf16[16,32,256]{2,1,0:T(8,128)(2,1)S(1)}, bf16[16,32,256]{2,1,0:T(8,128)(2,1)S(1)}, u32[]{:S(2)}, u32[]{:S(2)}) collective-permute-start(bf16[16,32,256]{2,1,0:T(8,128)(2,1)S(1)} %collective-permute-done.2.refs_1_), channel_id=1, source_target_pairs={{0,32},{32,64},{64,96},{96,0},{1,33},{33,65},{65,97},{97,1},{2,34}... | collective-permute-start | bytes 786440 | tf_op jit(solution)/shard_map/ppermute | solution.py:200
  63.1 0.3 shard_map.58
  63.4 0.1 collective-permute-start.1
  63.5 4.7 %collective-permute-done.5.refs_5_ = bf16[16,32,256]{2,1,0:T(8,128)(2,1)S(1)} collective-permute-done((bf16[16,32,256]{2,1,0:T(8,128)(2,1)S(1)}, bf16[16,32,256]{2,1,0:T(8,128)(2,1)S(1)}, u32[]{:S(2)}, u32[]{:S(2)}) %collective-permute-start.5) | collective-permute-done | bytes 262176 | tf_op jit(solution)/shard_map/ppermute | solution.py:200
  68.2 0.5 collective-permute-start.8
  68.7 1.4 %collective-permute-done.4.refs_3_ = bf16[16,32,256]{2,1,0:T(8,128)(2,1)S(1)} collective-permute-done((bf16[16,32,256]{2,1,0:T(8,128)(2,1)S(1)}, bf16[16,32,256]{2,1,0:T(8,128)(2,1)S(1)}, u32[]{:S(2)}, u32[]{:S(2)}) %collective-permute-start.4) | collective-permute-done | bytes 262176 | tf_op jit(solution)/shard_map/ppermute | solution.py:200
  70.1 2.8 %collective-permute-done.6.refs_6_ = bf16[16,32,256]{2,1,0:T(8,128)(2,1)S(1)} collective-permute-done((bf16[16,32,256]{2,1,0:T(8,128)(2,1)S(1)}, bf16[16,32,256]{2,1,0:T(8,128)(2,1)S(1)}, u32[]{:S(2)}, u32[]{:S(2)}) %collective-permute-start.6) | collective-permute-done | bytes 262176 | tf_op jit(solution)/shard_map/ppermute | solution.py:200
  72.9 0.5 collective-permute-start.10
  73.4 3.4 %copy-done.1 = bf16[1024,4096]{1,0:T(8,128)(2,1)S(1)} copy-done((bf16[1024,4096]{1,0:T(8,128)(2,1)S(1)}, bf16[1024,4096]{1,0:T(8,128)(2,1)}, u32[]{:S(2)}) %copy-start.1) | copy-done | bytes 8388632
  76.8 0.6 collective-permute-done.7
  77.4 0.6 collective-permute-start.13
  78.0 0.1 collective-permute-start.14
  78.1 0.4 collective-permute-start.15
  78.5 0.3 collective-permute-start.16
  78.8 0.1 collective-permute-done.12.refs_3_
  78.9 0.5 collective-permute-start.17
  79.5 2.7 %collective-permute-start.18 = (bf16[4,32,512]{2,1,0:T(8,128)(2,1)S(1)}, bf16[4,32,512]{2,1,0:T(8,128)(2,1)S(1)}, u32[]{:S(2)}, u32[]{:S(2)}) collective-permute-start(bf16[4,32,512]{2,1,0:T(8,128)(2,1)S(1)} %pad_maximum_fusion.refs_0_), channel_id=1, source_target_pairs={{0,96},{32,0},{64,32},{96,64},{1,97},{33,1},{65,33},{97,65},{2,98}... | collective-permute-start | bytes 393224 | tf_op jit(solution)/shard_map/ppermute | solution.py:200
  82.2 2.4 %shard_map.60.own_ref = f32[1024,256]{1,0:T(8,128)S(1)} custom-call(bf16[1024,4096]{1,0:T(8,128)(2,1)S(1)} %copy-done.1, bf16[16,128]{1,0:T(8,128)(2,1)S(1)} %shard_map.59.token_ref, bf16[16,32,256]{2,1,0:T(8,128)(2,1)S(1)} %all_to_all.16.sketch_ref.refs_0_, bf16[16,32,256]{2,1,0:T(8,128)(2,1)S(1)} %collective-permute-done.2.refs_1_, ...), custom_call_target="tpu_custom_call" | custom-call | tf_op jit(solution)/shard_map/pallas_call | solution.py:142
  84.6 2.4 %shard_map.61.other_ref = f32[1024,256]{1,0:T(8,128)S(1)} custom-call(bf16[1024,4096]{1,0:T(8,128)(2,1)S(1)} %copy-done.1, bf16[16,128]{1,0:T(8,128)(2,1)S(1)} %shard_map.59.token_ref, bf16[16,32,256]{2,1,0:T(8,128)(2,1)S(1)} %collective-permute-done.9.refs_0_, bf16[16,32,256]{2,1,0:T(8,128)(2,1)S(1)} %collective-permute-done.10.refs_1_, ...), custom_call_target="tpu_custom_call" | custom-call | tf_op jit(solution)/shard_map/pallas_call | solution.py:142
  87.0 0.8 collective-permute-done.18.refs_2_
  87.8 0.9 collective-permute-done.19.refs_3_
  88.7 2.4 %shard_map.62 = f32[16,1024]{1,0:T(8,128)} custom-call(s32[1]{0:T(128)} %bitcast.4.place_ref, f32[1024,256]{1,0:T(8,128)S(1)} %shard_map.60.own_ref, f32[1024,256]{1,0:T(8,128)S(1)} %shard_map.61.other_ref, bf16[1024,512]{1,0:T(8,128)(2,1)S(1)} %copy-done.3, bf16[4,32,512]{2,1,0:T(8,128)(2,1)S(1)} %pad_maximum_fusion.refs_0_, ...), custom_call_target="tpu_custom_call" | custom-call | flops 268435456 | bytes 1048576 | tf_op jit(solution)/shard_map/pallas_call | solution.py:188
  (34 shorter events, 0.2 us)
Async XLA Ops:
  0.0 0.8 copy-start
  0.8 40.8 %copy-start.2 = (bf16[1,256,4096]{2,1,0:T(8,128)(2,1)S(1)}, bf16[1,256,4096]{2,1,0:T(8,128)(2,1)}, u32[]{:S(2)}) copy-start(bf16[1,256,4096]{2,1,0:T(8,128)(2,1)} %acts_ref.1) | copy-start | bytes 6291460
  0.8 40.8 %copy-start.4 = (bf16[1,256,512]{2,1,0:T(8,128)(2,1)S(1)}, bf16[1,256,512]{2,1,0:T(8,128)(2,1)}, u32[]{:S(2)}) copy-start(bf16[1,256,512]{2,1,0:T(8,128)(2,1)} %grads_ref.2) | copy-start | bytes 786436
  43.3 19.8 %all-to-all-start.2 = ((bf16[16,32,512]{2,1,0:T(8,128)(2,1)}), bf16[16,32,512]{2,1,0:T(8,128)(2,1)S(1)}, u32[]{:S(2)}, u32[]{:S(2)}) async-start(bf16[16,32,512]{2,1,0:T(8,128)(2,1)} %get-tuple-element.41), calls=%async_computation.2 | async-start | bytes 1048576 | tf_op jit(solution)/shard_map/all_to_all | solution.py:28
  48.3 15.1 %collective-permute-start = (bf16[16,32,256]{2,1,0:T(8,128)(2,1)S(1)}, bf16[16,32,256]{2,1,0:T(8,128)(2,1)S(1)}, u32[]{:S(2)}, u32[]{:S(2)}) collective-permute-start(bf16[16,32,256]{2,1,0:T(8,128)(2,1)S(1)} %all_to_all.16.sketch_ref.refs_0_), channel_id=1, source_target_pairs={{0,96},{32,0},{64,32},{96,64},{1,97},{33,1},{65,33},{97,65},{2,98}... | collective-permute-start | bytes 786440 | tf_op jit(solution)/shard_map/ppermute | solution.py:200
  51.4 9.7 %collective-permute-start.2 = (bf16[16,32,256]{2,1,0:T(8,128)(2,1)S(1)}, bf16[16,32,256]{2,1,0:T(8,128)(2,1)S(1)}, u32[]{:S(2)}, u32[]{:S(2)}) collective-permute-start(bf16[16,32,256]{2,1,0:T(8,128)(2,1)S(1)} %all_to_all.16.sketch_ref.refs_0_), channel_id=1, source_target_pairs={{0,128},{128,0},{1,129},{129,1},{2,130},{130,2},{3,131},{131,3},{4... | collective-permute-start | bytes 786440 | tf_op jit(solution)/shard_map/ppermute | solution.py:200
  51.9 9.1 %collective-permute-start.3 = (bf16[16,32,256]{2,1,0:T(8,128)(2,1)S(1)}, bf16[16,32,256]{2,1,0:T(8,128)(2,1)S(1)}, u32[]{:S(2)}, u32[]{:S(2)}) collective-permute-start(bf16[16,32,256]{2,1,0:T(8,128)(2,1)S(1)} %all_to_all.16.sketch_ref.refs_0_), channel_id=1, source_target_pairs={{0,32},{32,64},{64,96},{96,0},{1,33},{33,65},{65,97},{97,1},{2,34}... | collective-permute-start | bytes 786440 | tf_op jit(solution)/shard_map/ppermute | solution.py:200
  61.1 7.1 %collective-permute-start.5 = (bf16[16,32,256]{2,1,0:T(8,128)(2,1)S(1)}, bf16[16,32,256]{2,1,0:T(8,128)(2,1)S(1)}, u32[]{:S(2)}, u32[]{:S(2)}) collective-permute-start(bf16[16,32,256]{2,1,0:T(8,128)(2,1)S(1)} %collective-permute-done.2.refs_1_), channel_id=1, source_target_pairs={{0,96},{32,0},{64,32},{96,64},{1,97},{33,1},{65,33},{97,65},{2,98}... | collective-permute-start | bytes 786440 | tf_op jit(solution)/shard_map/ppermute | solution.py:200
  61.1 9.0 %collective-permute-start.4 = (bf16[16,32,256]{2,1,0:T(8,128)(2,1)S(1)}, bf16[16,32,256]{2,1,0:T(8,128)(2,1)S(1)}, u32[]{:S(2)}, u32[]{:S(2)}) collective-permute-start(bf16[16,32,256]{2,1,0:T(8,128)(2,1)S(1)} %collective-permute-done.2.refs_1_), channel_id=1, source_target_pairs={{0,32},{32,64},{64,96},{96,0},{1,33},{33,65},{65,97},{97,1},{2,34}... | collective-permute-start | bytes 786440 | tf_op jit(solution)/shard_map/ppermute | solution.py:200
  63.1 9.8 %collective-permute-start.6 = (bf16[16,32,256]{2,1,0:T(8,128)(2,1)S(1)}, bf16[16,32,256]{2,1,0:T(8,128)(2,1)S(1)}, u32[]{:S(2)}, u32[]{:S(2)}) collective-permute-start(bf16[16,32,256]{2,1,0:T(8,128)(2,1)S(1)} %collective-permute-done.3.refs_2_), channel_id=1, source_target_pairs={{0,32},{32,64},{64,96},{96,0},{1,33},{33,65},{65,97},{97,1},{2,34}... | collective-permute-start | bytes 786440 | tf_op jit(solution)/shard_map/ppermute | solution.py:200
  63.4 5.2 %collective-permute-start.1 = (bf16[32,512]{1,0:T(8,128)(2,1)S(1)}, bf16[32,512]{1,0:T(8,128)(2,1)S(1)}, u32[]{:S(2)}, u32[]{:S(2)}) collective-permute-start(bf16[32,512]{1,0:T(8,128)(2,1)S(1)} %shard_map.58), channel_id=1, source_target_pairs={{0,16},{16,0},{1,17},{17,1},{2,18},{18,2},{3,19},{19,3},{4,20},{20... | collective-permute-start | bytes 98312 | tf_op jit(solution)/shard_map/ppermute | solution.py:32
  68.2 9.2 %collective-permute-start.8 = (bf16[16,32,256]{2,1,0:T(8,128)(2,1)S(1)}, bf16[16,32,256]{2,1,0:T(8,128)(2,1)S(1)}, u32[]{:S(2)}, u32[]{:S(2)}) collective-permute-start(bf16[16,32,256]{2,1,0:T(8,128)(2,1)S(1)} %collective-permute-done.5.refs_5_), channel_id=1, source_target_pairs={{0,96},{32,0},{64,32},{96,64},{1,97},{33,1},{65,33},{97,65},{2,98}... | collective-permute-start | bytes 786440 | tf_op jit(solution)/shard_map/ppermute | solution.py:200
  72.9 5.1 %collective-permute-start.9 = (bf16[16,32,256]{2,1,0:T(8,128)(2,1)S(1)}, bf16[16,32,256]{2,1,0:T(8,128)(2,1)S(1)}, u32[]{:S(2)}, u32[]{:S(2)}) collective-permute-start(bf16[16,32,256]{2,1,0:T(8,128)(2,1)S(1)} %all_to_all.16.sketch_ref.refs_0_), channel_id=1, source_target_pairs={{0,16},{16,0},{1,17},{17,1},{2,18},{18,2},{3,19},{19,3},{4,20},{20... | collective-permute-start | bytes 786440 | tf_op jit(solution)/shard_map/ppermute | solution.py:32
  72.9 4.5 %collective-permute-start.7 = (bf16[2,32,512]{2,1,0:T(8,128)(2,1)S(1)}, bf16[2,32,512]{2,1,0:T(8,128)(2,1)S(1)}, u32[]{:S(2)}, u32[]{:S(2)}) collective-permute-start(bf16[2,32,512]{2,1,0:T(8,128)(2,1)S(1)} %pad_maximum_fusion.1), channel_id=1, source_target_pairs={{0,128},{128,0},{1,129},{129,1},{2,130},{130,2},{3,131},{131,3},{4... | collective-permute-start | bytes 196616 | tf_op jit(solution)/shard_map/ppermute | solution.py:200
  72.9 5.2 %collective-permute-start.10 = (bf16[16,32,256]{2,1,0:T(8,128)(2,1)S(1)}, bf16[16,32,256]{2,1,0:T(8,128)(2,1)S(1)}, u32[]{:S(2)}, u32[]{:S(2)}) collective-permute-start(bf16[16,32,256]{2,1,0:T(8,128)(2,1)S(1)} %collective-permute-done.2.refs_1_), channel_id=1, source_target_pairs={{0,16},{16,0},{1,17},{17,1},{2,18},{18,2},{3,19},{19,3},{4,20},{20... | collective-permute-start | bytes 786440 | tf_op jit(solution)/shard_map/ppermute | solution.py:32
  73.4 5.1 %collective-permute-start.11 = (bf16[16,32,256]{2,1,0:T(8,128)(2,1)S(1)}, bf16[16,32,256]{2,1,0:T(8,128)(2,1)S(1)}, u32[]{:S(2)}, u32[]{:S(2)}) collective-permute-start(bf16[16,32,256]{2,1,0:T(8,128)(2,1)S(1)} %collective-permute-done.3.refs_2_), channel_id=1, source_target_pairs={{0,16},{16,0},{1,17},{17,1},{2,18},{18,2},{3,19},{19,3},{4,20},{20... | collective-permute-start | bytes 786440 | tf_op jit(solution)/shard_map/ppermute | solution.py:32
  73.4 3.4 %copy-start.1 = (bf16[1024,4096]{1,0:T(8,128)(2,1)S(1)}, bf16[1024,4096]{1,0:T(8,128)(2,1)}, u32[]{:S(2)}) copy-start(bf16[1024,4096]{1,0:T(8,128)(2,1)} %acts_ref.4) | copy-start | bytes 25165828
  77.4 1.5 %collective-permute-start.12 = (bf16[16,32,256]{2,1,0:T(8,128)(2,1)S(1)}, bf16[16,32,256]{2,1,0:T(8,128)(2,1)S(1)}, u32[]{:S(2)}, u32[]{:S(2)}) collective-permute-start(bf16[16,32,256]{2,1,0:T(8,128)(2,1)S(1)} %collective-permute-done.4.refs_3_), channel_id=1, source_target_pairs={{0,16},{16,0},{1,17},{17,1},{2,18},{18,2},{3,19},{19,3},{4,20},{20... | collective-permute-start | bytes 786440 | tf_op jit(solution)/shard_map/ppermute | solution.py:32
  77.4 2.0 %collective-permute-start.13 = (bf16[16,32,256]{2,1,0:T(8,128)(2,1)S(1)}, bf16[16,32,256]{2,1,0:T(8,128)(2,1)S(1)}, u32[]{:S(2)}, u32[]{:S(2)}) collective-permute-start(bf16[16,32,256]{2,1,0:T(8,128)(2,1)S(1)} %collective-permute-done.refs_4_), channel_id=1, source_target_pairs={{0,16},{16,0},{1,17},{17,1},{2,18},{18,2},{3,19},{19,3},{4,20},{20... | collective-permute-start | bytes 786440 | tf_op jit(solution)/shard_map/ppermute | solution.py:32
  78.0 4.2 %collective-permute-start.14 = (bf16[16,32,256]{2,1,0:T(8,128)(2,1)S(1)}, bf16[16,32,256]{2,1,0:T(8,128)(2,1)S(1)}, u32[]{:S(2)}, u32[]{:S(2)}) collective-permute-start(bf16[16,32,256]{2,1,0:T(8,128)(2,1)S(1)} %collective-permute-done.5.refs_5_), channel_id=1, source_target_pairs={{0,16},{16,0},{1,17},{17,1},{2,18},{18,2},{3,19},{19,3},{4,20},{20... | collective-permute-start | bytes 786440 | tf_op jit(solution)/shard_map/ppermute | solution.py:32
  78.1 6.4 %collective-permute-start.15 = (bf16[16,32,256]{2,1,0:T(8,128)(2,1)S(1)}, bf16[16,32,256]{2,1,0:T(8,128)(2,1)S(1)}, u32[]{:S(2)}, u32[]{:S(2)}) collective-permute-start(bf16[16,32,256]{2,1,0:T(8,128)(2,1)S(1)} %collective-permute-done.6.refs_6_), channel_id=1, source_target_pairs={{0,16},{16,0},{1,17},{17,1},{2,18},{18,2},{3,19},{19,3},{4,20},{20... | collective-permute-start | bytes 786440 | tf_op jit(solution)/shard_map/ppermute | solution.py:32
  78.5 6.0 %collective-permute-start.16 = (bf16[16,32,256]{2,1,0:T(8,128)(2,1)S(1)}, bf16[16,32,256]{2,1,0:T(8,128)(2,1)S(1)}, u32[]{:S(2)}, u32[]{:S(2)}) collective-permute-start(bf16[16,32,256]{2,1,0:T(8,128)(2,1)S(1)} %collective-permute-done.8.refs_7_), channel_id=1, source_target_pairs={{0,16},{16,0},{1,17},{17,1},{2,18},{18,2},{3,19},{19,3},{4,20},{20... | collective-permute-start | bytes 786440 | tf_op jit(solution)/shard_map/ppermute | solution.py:32
  78.9 8.0 %collective-permute-start.17 = (bf16[4,32,512]{2,1,0:T(8,128)(2,1)S(1)}, bf16[4,32,512]{2,1,0:T(8,128)(2,1)S(1)}, u32[]{:S(2)}, u32[]{:S(2)}) collective-permute-start(bf16[4,32,512]{2,1,0:T(8,128)(2,1)S(1)} %pad_maximum_fusion.refs_0_), channel_id=1, source_target_pairs={{0,32},{32,64},{64,96},{96,0},{1,33},{33,65},{65,97},{97,1},{2,34}... | collective-permute-start | bytes 393224 | tf_op jit(solution)/shard_map/ppermute | solution.py:200
  79.5 8.3 %collective-permute-start.18 = (bf16[4,32,512]{2,1,0:T(8,128)(2,1)S(1)}, bf16[4,32,512]{2,1,0:T(8,128)(2,1)S(1)}, u32[]{:S(2)}, u32[]{:S(2)}) collective-permute-start(bf16[4,32,512]{2,1,0:T(8,128)(2,1)S(1)} %pad_maximum_fusion.refs_0_), channel_id=1, source_target_pairs={{0,96},{32,0},{64,32},{96,64},{1,97},{33,1},{65,33},{97,65},{2,98}... | collective-permute-start | bytes 393224 | tf_op jit(solution)/shard_map/ppermute | solution.py:200
  82.2 6.5 %collective-permute-start.19 = (bf16[4,32,512]{2,1,0:T(8,128)(2,1)S(1)}, bf16[4,32,512]{2,1,0:T(8,128)(2,1)S(1)}, u32[]{:S(2)}, u32[]{:S(2)}) collective-permute-start(bf16[4,32,512]{2,1,0:T(8,128)(2,1)S(1)} %pad_maximum_fusion.refs_0_), channel_id=1, source_target_pairs={{0,64},{32,96},{64,0},{96,32},{1,65},{33,97},{65,1},{97,33},{2,66}... | collective-permute-start | bytes 393224 | tf_op jit(solution)/shard_map/ppermute | solution.py:200
  84.5 4.1 %copy-start.3 = (bf16[1024,512]{1,0:T(8,128)(2,1)S(1)}, bf16[1024,512]{1,0:T(8,128)(2,1)}, u32[]{:S(2)}) copy-start(bf16[1024,512]{1,0:T(8,128)(2,1)} %grads_ref.3) | copy-start | bytes 3145732

commit v5 on v4

--- a/solution.py
+++ b/solution.py
@@ -229,9 +229,8 @@
     early = [sketch, beside, behind, corners[0], ahead, corners[1], across[0]]
     both, acts, *early = lax.optimization_barrier((both, res_acts, *early))
     both = jnp.concatenate([both, from_back(both, "xlo", 1)])
-    other_early = [swap_cores(block) for block in early[:4]]
-    both, token, *later = lax.optimization_barrier((both, touch(acts), *early[4:]))
-    other_early += [swap_cores(block) for block in later]
+    other_early = [swap_cores(block) for block in early]
+    both, token = lax.optimization_barrier((both, touch(acts)))
     rights = [both] + [from_back(both, "y", step) for step in (1, 3, 2)]
     token, last, *early = lax.optimization_barrier((token, across[1], *early))
     own_left = on_left(early + [last], acts, token)

time: 91.7 us -> 95.1 us (1.037)
  waiting for transfers between devices: 17.8 us -> 21.5 us
    ppermute x11, waiting for transfers between devices: 17.6 us -> 21.5 us  [from_back(): lax.ppermute(block, axis, [(i, (i + step) % size) for i in range(size)])]
where the time goes in v5:
time: 95.1 us; the launch traced here: 94.7 us
  blocking collectives  38.1 us (40%)
  waiting for transfers between devices  21.5 us (23%)
  starting transfers between devices  16.3 us (17%)
  Pallas kernels  11.9 us (13%)
  local copies, waits for them, and re-layouts  4.19 us (4%)
  matrix products  2.54 us (3%)
    all_to_all x2, blocking collectives, exchange(): return lax.all_to_all(blocks, axes, 0, 0, tiled=True)  38.1 us
    ppermute x11, waiting for transfers between devices, from_back(): lax.ppermute(block, axis, [(i, (i + step) % size) for i in range(size)])  21.5 us
    ppermute x11, starting transfers between devices, from_back(): lax.ppermute(block, axis, [(i, (i + step) % size) for i in range(size)])  9.38 us
    all_to_all x1, starting transfers between devices, exchange(): return lax.all_to_all(blocks, axes, 0, 0, tiled=True)  5 us
    pallas_call x2, Pallas kernels, on_left(): pl.pallas_call(left_kernel, in_specs=[pl.BlockSpec(memory_space=pltpu.VME...  4.73 us
    unnamed x10, local copies, waits for them, and re-layouts  4.15 us
    pallas_call x1, Pallas kernels, invert(): pl.pallas_call(inverse_kernel, out_shape=jax.ShapeDtypeStruct(gram.shape,...  2.68 us
    dot_general x1, matrix products, partial_sketch(): jnp.dot(projected, query_acts[0], preferred_element_type=F32).astype(BF16)  2.54 us
  transfers between devices with their start and end apart: 21, of which 8 were waited for; matrix products, arithmetic and copies ran while one was open for 0% of the time, Pallas kernels for 8%

profile of v5, /device:TPU:32, one launch (start us, length us, event | category | flops | bytes accessed | tf_op | source)
XLA Modules:
  0.0 94.7 jit_solution(5152976409216697462)
XLA Ops:
  0.0 0.8 copy-done
  0.8 2.5 %convolution_convert_fusion = bf16[32,4096]{1,0:T(8,128)(2,1)S(1)} fusion(bf16[1,256,4096]{2,1,0:T(8,128)(2,1)} %acts_ref.1, bf16[1,256,512]{2,1,0:T(8,128)(2,1)} %grads_ref.2, bf16[1,32,512]{2,1,0:T(8,128)(2,1)S(1)} %copy-done), kind=kOutput, calls=%fused_computation | convolution fusion | flops 75636736 | bytes 2654208 | tf_op jit(solution)/shard_map/dot_general | solution.py:42
  3.4 23.0 %all_to_all.15.parts_ref = bf16[16,32,256]{2,1,0:T(8,128)(2,1)S(1)} all-to-all(bf16[16,32,256]{2,1,0:T(8,128)(2,1)S(1)} %bitcast.22), channel_id=1, replica_groups=mesh['xlo'=2,'y'=4,'core'=2,'z'=8,'xhi'=2] {'z','xhi'}, dimensions={0} | all-to-all | bytes 524288 | tf_op jit(solution)/shard_map/all_to_all | solution.py:28
  26.4 15.1 %all_to_all.16.sketch_ref.refs_0_ = bf16[16,32,256]{2,1,0:T(8,128)(2,1)S(1)} all-to-all(bf16[16,32,256]{2,1,0:T(8,128)(2,1)S(1)} %shard_map.55), channel_id=1, replica_groups=mesh['xlo'=2,'y'=4,'core'=2,'z'=8,'xhi'=2] {'z','xhi'}, dimensions={0} | all-to-all | bytes 524288 | tf_op jit(solution)/shard_map/all_to_all | solution.py:28
  41.5 1.8 %shard_map.56 = (bf16[16,32,512]{2,1,0:T(8,128)(2,1)}, f32[32,32]{1,0:T(8,128)S(1)}) custom-call(bf16[16,32,256]{2,1,0:T(8,128)(2,1)S(1)} %all_to_all.16.sketch_ref.refs_0_, bf16[1,256,4096]{2,1,0:T(8,128)(2,1)S(1)} %copy-done.2, bf16[1,256,512]{2,1,0:T(8,128)(2,1)S(1)} %copy-done.4), custom_call_target="tpu_custom_call" | custom-call | flops 75497472 | bytes 2097152 | tf_op jit(solution)/shard_map/pallas_call | solution.py:72
  43.3 5.0 %all-to-all-start.2 = ((bf16[16,32,512]{2,1,0:T(8,128)(2,1)}), bf16[16,32,512]{2,1,0:T(8,128)(2,1)S(1)}, u32[]{:S(2)}, u32[]{:S(2)}) async-start(bf16[16,32,512]{2,1,0:T(8,128)(2,1)} %get-tuple-element.38), calls=%async_computation.2 | async-start | bytes 1048576 | tf_op jit(solution)/shard_map/all_to_all | solution.py:28
  48.3 3.0 %collective-permute-start = (bf16[16,32,256]{2,1,0:T(8,128)(2,1)S(1)}, bf16[16,32,256]{2,1,0:T(8,128)(2,1)S(1)}, u32[]{:S(2)}, u32[]{:S(2)}) collective-permute-start(bf16[16,32,256]{2,1,0:T(8,128)(2,1)S(1)} %all_to_all.16.sketch_ref.refs_0_), channel_id=1, source_target_pairs={{0,96},{32,0},{64,32},{96,64},{1,97},{33,1},{65,33},{97,65},{2,98}... | collective-permute-start | bytes 786440 | tf_op jit(solution)/shard_map/ppermute | solution.py:200
  51.4 0.6 collective-permute-start.2
  51.9 2.7 %shard_map.57.inverse_ref = f32[32,32]{1,0:T(8,128)S(1)} custom-call(f32[32,32]{1,0:T(8,128)S(1)} %get-tuple-element.39.gram_ref), custom_call_target="tpu_custom_call" | custom-call | flops 4294967296 | bytes 4194304 | tf_op jit(solution)/shard_map/pallas_call | solution.py:98
  54.6 6.4 %collective-permute-done.2.refs_1_ = bf16[16,32,256]{2,1,0:T(8,128)(2,1)S(1)} collective-permute-done((bf16[16,32,256]{2,1,0:T(8,128)(2,1)S(1)}, bf16[16,32,256]{2,1,0:T(8,128)(2,1)S(1)}, u32[]{:S(2)}, u32[]{:S(2)}) %collective-permute-start.2) | collective-permute-done | bytes 262176 | tf_op jit(solution)/shard_map/ppermute | solution.py:200
  61.1 2.0 %collective-permute-start.4 = (bf16[16,32,256]{2,1,0:T(8,128)(2,1)S(1)}, bf16[16,32,256]{2,1,0:T(8,128)(2,1)S(1)}, u32[]{:S(2)}, u32[]{:S(2)}) collective-permute-start(bf16[16,32,256]{2,1,0:T(8,128)(2,1)S(1)} %collective-permute-done.2.refs_1_), channel_id=1, source_target_pairs={{0,32},{32,64},{64,96},{96,0},{1,33},{33,65},{65,97},{97,1},{2,34}... | collective-permute-start | bytes 786440 | tf_op jit(solution)/shard_map/ppermute | solution.py:200
  63.1 0.0 collective-permute-start.6
  63.1 0.3 shard_map.58
  63.4 0.1 collective-permute-start.1
  63.5 4.7 %collective-permute-done.5.refs_5_ = bf16[16,32,256]{2,1,0:T(8,128)(2,1)S(1)} collective-permute-done((bf16[16,32,256]{2,1,0:T(8,128)(2,1)S(1)}, bf16[16,32,256]{2,1,0:T(8,128)(2,1)S(1)}, u32[]{:S(2)}, u32[]{:S(2)}) %collective-permute-start.5) | collective-permute-done | bytes 262176 | tf_op jit(solution)/shard_map/ppermute | solution.py:200
  68.2 0.5 collective-permute-start.8
  68.7 1.4 %collective-permute-done.4.refs_3_ = bf16[16,32,256]{2,1,0:T(8,128)(2,1)S(1)} collective-permute-done((bf16[16,32,256]{2,1,0:T(8,128)(2,1)S(1)}, bf16[16,32,256]{2,1,0:T(8,128)(2,1)S(1)}, u32[]{:S(2)}, u32[]{:S(2)}) %collective-permute-start.4) | collective-permute-done | bytes 262176 | tf_op jit(solution)/shard_map/ppermute | solution.py:200
  70.1 2.8 %collective-permute-done.6.refs_6_ = bf16[16,32,256]{2,1,0:T(8,128)(2,1)S(1)} collective-permute-done((bf16[16,32,256]{2,1,0:T(8,128)(2,1)S(1)}, bf16[16,32,256]{2,1,0:T(8,128)(2,1)S(1)}, u32[]{:S(2)}, u32[]{:S(2)}) %collective-permute-start.6) | collective-permute-done | bytes 262176 | tf_op jit(solution)/shard_map/ppermute | solution.py:200
  72.9 0.5 collective-permute-start.10
  73.4 1.2 %collective-permute-done.8.refs_7_ = bf16[16,32,256]{2,1,0:T(8,128)(2,1)S(1)} collective-permute-done((bf16[16,32,256]{2,1,0:T(8,128)(2,1)S(1)}, bf16[16,32,256]{2,1,0:T(8,128)(2,1)S(1)}, u32[]{:S(2)}, u32[]{:S(2)}) %collective-permute-start.8) | collective-permute-done | bytes 262176 | tf_op jit(solution)/shard_map/ppermute | solution.py:200
  74.6 3.3 %collective-permute-done.7 = bf16[2,32,512]{2,1,0:T(8,128)(2,1)S(1)} collective-permute-done((bf16[2,32,512]{2,1,0:T(8,128)(2,1)S(1)}, bf16[2,32,512]{2,1,0:T(8,128)(2,1)S(1)}, u32[]{:S(2)}, u32[]{:S(2)}) %collective-permute-start.7) | collective-permute-done | bytes 65568 | tf_op jit(solution)/shard_map/ppermute | solution.py:200
  77.9 0.5 collective-permute-start.14
  78.4 3.4 %copy-done.1 = bf16[1024,4096]{1,0:T(8,128)(2,1)S(1)} copy-done((bf16[1024,4096]{1,0:T(8,128)(2,1)S(1)}, bf16[1024,4096]{1,0:T(8,128)(2,1)}, u32[]{:S(2)}) %copy-start.1) | copy-done | bytes 8388632
  81.8 0.3 collective-permute-start.15
  82.1 0.5 collective-permute-start.16
  82.6 0.5 collective-permute-start.17
  83.2 2.7 %collective-permute-start.18 = (bf16[4,32,512]{2,1,0:T(8,128)(2,1)S(1)}, bf16[4,32,512]{2,1,0:T(8,128)(2,1)S(1)}, u32[]{:S(2)}, u32[]{:S(2)}) collective-permute-start(bf16[4,32,512]{2,1,0:T(8,128)(2,1)S(1)} %pad_maximum_fusion.refs_0_), channel_id=1, source_target_pairs={{0,96},{32,0},{64,32},{96,64},{1,97},{33,1},{65,33},{97,65},{2,98}... | collective-permute-start | bytes 393224 | tf_op jit(solution)/shard_map/ppermute | solution.py:200
  85.9 2.4 %shard_map.60.own_ref = f32[1024,256]{1,0:T(8,128)S(1)} custom-call(bf16[1024,4096]{1,0:T(8,128)(2,1)S(1)} %copy-done.1, bf16[16,128]{1,0:T(8,128)(2,1)S(1)} %shard_map.59.token_ref, bf16[16,32,256]{2,1,0:T(8,128)(2,1)S(1)} %all_to_all.16.sketch_ref.refs_0_, bf16[16,32,256]{2,1,0:T(8,128)(2,1)S(1)} %collective-permute-done.2.refs_1_, ...), custom_call_target="tpu_custom_call" | custom-call | tf_op jit(solution)/shard_map/pallas_call | solution.py:142
  88.3 2.4 %shard_map.61.other_ref = f32[1024,256]{1,0:T(8,128)S(1)} custom-call(bf16[1024,4096]{1,0:T(8,128)(2,1)S(1)} %copy-done.1, bf16[16,128]{1,0:T(8,128)(2,1)S(1)} %shard_map.59.token_ref, bf16[16,32,256]{2,1,0:T(8,128)(2,1)S(1)} %collective-permute-done.9.refs_0_, bf16[16,32,256]{2,1,0:T(8,128)(2,1)S(1)} %collective-permute-done.10.refs_1_, ...), custom_call_target="tpu_custom_call" | custom-call | tf_op jit(solution)/shard_map/pallas_call | solution.py:142
  90.7 0.8 collective-permute-done.18.refs_2_
  91.5 0.9 collective-permute-done.19.refs_3_
  92.3 2.4 %shard_map.62 = f32[16,1024]{1,0:T(8,128)} custom-call(s32[1]{0:T(128)} %bitcast.4.place_ref, f32[1024,256]{1,0:T(8,128)S(1)} %shard_map.60.own_ref, f32[1024,256]{1,0:T(8,128)S(1)} %shard_map.61.other_ref, bf16[1024,512]{1,0:T(8,128)(2,1)S(1)} %copy-done.3, bf16[4,32,512]{2,1,0:T(8,128)(2,1)S(1)} %pad_maximum_fusion.refs_0_, ...), custom_call_target="tpu_custom_call" | custom-call | flops 268435456 | bytes 1048576 | tf_op jit(solution)/shard_map/pallas_call | solution.py:188
  (34 shorter events, 0.2 us)
Async XLA Ops:
  0.0 0.8 copy-start
  0.8 40.8 %copy-start.2 = (bf16[1,256,4096]{2,1,0:T(8,128)(2,1)S(1)}, bf16[1,256,4096]{2,1,0:T(8,128)(2,1)}, u32[]{:S(2)}) copy-start(bf16[1,256,4096]{2,1,0:T(8,128)(2,1)} %acts_ref.1) | copy-start | bytes 6291460
  0.8 40.8 %copy-start.4 = (bf16[1,256,512]{2,1,0:T(8,128)(2,1)S(1)}, bf16[1,256,512]{2,1,0:T(8,128)(2,1)}, u32[]{:S(2)}) copy-start(bf16[1,256,512]{2,1,0:T(8,128)(2,1)} %grads_ref.2) | copy-start | bytes 786436
  43.3 19.8 %all-to-all-start.2 = ((bf16[16,32,512]{2,1,0:T(8,128)(2,1)}), bf16[16,32,512]{2,1,0:T(8,128)(2,1)S(1)}, u32[]{:S(2)}, u32[]{:S(2)}) async-start(bf16[16,32,512]{2,1,0:T(8,128)(2,1)} %get-tuple-element.38), calls=%async_computation.2 | async-start | bytes 1048576 | tf_op jit(solution)/shard_map/all_to_all | solution.py:28
  48.3 15.1 %collective-permute-start = (bf16[16,32,256]{2,1,0:T(8,128)(2,1)S(1)}, bf16[16,32,256]{2,1,0:T(8,128)(2,1)S(1)}, u32[]{:S(2)}, u32[]{:S(2)}) collective-permute-start(bf16[16,32,256]{2,1,0:T(8,128)(2,1)S(1)} %all_to_all.16.sketch_ref.refs_0_), channel_id=1, source_target_pairs={{0,96},{32,0},{64,32},{96,64},{1,97},{33,1},{65,33},{97,65},{2,98}... | collective-permute-start | bytes 786440 | tf_op jit(solution)/shard_map/ppermute | solution.py:200
  51.4 9.7 %collective-permute-start.2 = (bf16[16,32,256]{2,1,0:T(8,128)(2,1)S(1)}, bf16[16,32,256]{2,1,0:T(8,128)(2,1)S(1)}, u32[]{:S(2)}, u32[]{:S(2)}) collective-permute-start(bf16[16,32,256]{2,1,0:T(8,128)(2,1)S(1)} %all_to_all.16.sketch_ref.refs_0_), channel_id=1, source_target_pairs={{0,128},{128,0},{1,129},{129,1},{2,130},{130,2},{3,131},{131,3},{4... | collective-permute-start | bytes 786440 | tf_op jit(solution)/shard_map/ppermute | solution.py:200
  51.9 9.1 %collective-permute-start.3 = (bf16[16,32,256]{2,1,0:T(8,128)(2,1)S(1)}, bf16[16,32,256]{2,1,0:T(8,128)(2,1)S(1)}, u32[]{:S(2)}, u32[]{:S(2)}) collective-permute-start(bf16[16,32,256]{2,1,0:T(8,128)(2,1)S(1)} %all_to_all.16.sketch_ref.refs_0_), channel_id=1, source_target_pairs={{0,32},{32,64},{64,96},{96,0},{1,33},{33,65},{65,97},{97,1},{2,34}... | collective-permute-start | bytes 786440 | tf_op jit(solution)/shard_map/ppermute | solution.py:200
  61.1 7.1 %collective-permute-start.5 = (bf16[16,32,256]{2,1,0:T(8,128)(2,1)S(1)}, bf16[16,32,256]{2,1,0:T(8,128)(2,1)S(1)}, u32[]{:S(2)}, u32[]{:S(2)}) collective-permute-start(bf16[16,32,256]{2,1,0:T(8,128)(2,1)S(1)} %collective-permute-done.2.refs_1_), channel_id=1, source_target_pairs={{0,96},{32,0},{64,32},{96,64},{1,97},{33,1},{65,33},{97,65},{2,98}... | collective-permute-start | bytes 786440 | tf_op jit(solution)/shard_map/ppermute | solution.py:200
  61.1 9.0 %collective-permute-start.4 = (bf16[16,32,256]{2,1,0:T(8,128)(2,1)S(1)}, bf16[16,32,256]{2,1,0:T(8,128)(2,1)S(1)}, u32[]{:S(2)}, u32[]{:S(2)}) collective-permute-start(bf16[16,32,256]{2,1,0:T(8,128)(2,1)S(1)} %collective-permute-done.2.refs_1_), channel_id=1, source_target_pairs={{0,32},{32,64},{64,96},{96,0},{1,33},{33,65},{65,97},{97,1},{2,34}... | collective-permute-start | bytes 786440 | tf_op jit(solution)/shard_map/ppermute | solution.py:200
  63.1 9.8 %collective-permute-start.6 = (bf16[16,32,256]{2,1,0:T(8,128)(2,1)S(1)}, bf16[16,32,256]{2,1,0:T(8,128)(2,1)S(1)}, u32[]{:S(2)}, u32[]{:S(2)}) collective-permute-start(bf16[16,32,256]{2,1,0:T(8,128)(2,1)S(1)} %collective-permute-done.3.refs_2_), channel_id=1, source_target_pairs={{0,32},{32,64},{64,96},{96,0},{1,33},{33,65},{65,97},{97,1},{2,34}... | collective-permute-start | bytes 786440 | tf_op jit(solution)/shard_map/ppermute | solution.py:200
  63.4 5.2 %collective-permute-start.1 = (bf16[32,512]{1,0:T(8,128)(2,1)S(1)}, bf16[32,512]{1,0:T(8,128)(2,1)S(1)}, u32[]{:S(2)}, u32[]{:S(2)}) collective-permute-start(bf16[32,512]{1,0:T(8,128)(2,1)S(1)} %shard_map.58), channel_id=1, source_target_pairs={{0,16},{16,0},{1,17},{17,1},{2,18},{18,2},{3,19},{19,3},{4,20},{20... | collective-permute-start | bytes 98312 | tf_op jit(solution)/shard_map/ppermute | solution.py:32
  68.2 6.4 %collective-permute-start.8 = (bf16[16,32,256]{2,1,0:T(8,128)(2,1)S(1)}, bf16[16,32,256]{2,1,0:T(8,128)(2,1)S(1)}, u32[]{:S(2)}, u32[]{:S(2)}) collective-permute-start(bf16[16,32,256]{2,1,0:T(8,128)(2,1)S(1)} %collective-permute-done.5.refs_5_), channel_id=1, source_target_pairs={{0,96},{32,0},{64,32},{96,64},{1,97},{33,1},{65,33},{97,65},{2,98}... | collective-permute-start | bytes 786440 | tf_op jit(solution)/shard_map/ppermute | solution.py:200
  72.9 5.0 %collective-permute-start.9 = (bf16[16,32,256]{2,1,0:T(8,128)(2,1)S(1)}, bf16[16,32,256]{2,1,0:T(8,128)(2,1)S(1)}, u32[]{:S(2)}, u32[]{:S(2)}) collective-permute-start(bf16[16,32,256]{2,1,0:T(8,128)(2,1)S(1)} %all_to_all.16.sketch_ref.refs_0_), channel_id=1, source_target_pairs={{0,16},{16,0},{1,17},{17,1},{2,18},{18,2},{3,19},{19,3},{4,20},{20... | collective-permute-start | bytes 786440 | tf_op jit(solution)/shard_map/ppermute | solution.py:32
  72.9 8.9 %collective-permute-start.10 = (bf16[16,32,256]{2,1,0:T(8,128)(2,1)S(1)}, bf16[16,32,256]{2,1,0:T(8,128)(2,1)S(1)}, u32[]{:S(2)}, u32[]{:S(2)}) collective-permute-start(bf16[16,32,256]{2,1,0:T(8,128)(2,1)S(1)} %collective-permute-done.2.refs_1_), channel_id=1, source_target_pairs={{0,16},{16,0},{1,17},{17,1},{2,18},{18,2},{3,19},{19,3},{4,20},{20... | collective-permute-start | bytes 786440 | tf_op jit(solution)/shard_map/ppermute | solution.py:32
  73.4 8.7 %collective-permute-start.11 = (bf16[16,32,256]{2,1,0:T(8,128)(2,1)S(1)}, bf16[16,32,256]{2,1,0:T(8,128)(2,1)S(1)}, u32[]{:S(2)}, u32[]{:S(2)}) collective-permute-start(bf16[16,32,256]{2,1,0:T(8,128)(2,1)S(1)} %collective-permute-done.3.refs_2_), channel_id=1, source_target_pairs={{0,16},{16,0},{1,17},{17,1},{2,18},{18,2},{3,19},{19,3},{4,20},{20... | collective-permute-start | bytes 786440 | tf_op jit(solution)/shard_map/ppermute | solution.py:32
  73.4 4.5 %collective-permute-start.7 = (bf16[2,32,512]{2,1,0:T(8,128)(2,1)S(1)}, bf16[2,32,512]{2,1,0:T(8,128)(2,1)S(1)}, u32[]{:S(2)}, u32[]{:S(2)}) collective-permute-start(bf16[2,32,512]{2,1,0:T(8,128)(2,1)S(1)} %pad_maximum_fusion.1), channel_id=1, source_target_pairs={{0,128},{128,0},{1,129},{129,1},{2,130},{130,2},{3,131},{131,3},{4... | collective-permute-start | bytes 196616 | tf_op jit(solution)/shard_map/ppermute | solution.py:200
  74.6 8.0 %collective-permute-start.12 = (bf16[16,32,256]{2,1,0:T(8,128)(2,1)S(1)}, bf16[16,32,256]{2,1,0:T(8,128)(2,1)S(1)}, u32[]{:S(2)}, u32[]{:S(2)}) collective-permute-start(bf16[16,32,256]{2,1,0:T(8,128)(2,1)S(1)} %collective-permute-done.4.refs_3_), channel_id=1, source_target_pairs={{0,16},{16,0},{1,17},{17,1},{2,18},{18,2},{3,19},{19,3},{4,20},{20... | collective-permute-start | bytes 786440 | tf_op jit(solution)/shard_map/ppermute | solution.py:32
  77.9 5.2 %collective-permute-start.13 = (bf16[16,32,256]{2,1,0:T(8,128)(2,1)S(1)}, bf16[16,32,256]{2,1,0:T(8,128)(2,1)S(1)}, u32[]{:S(2)}, u32[]{:S(2)}) collective-permute-start(bf16[16,32,256]{2,1,0:T(8,128)(2,1)S(1)} %collective-permute-done.refs_4_), channel_id=1, source_target_pairs={{0,16},{16,0},{1,17},{17,1},{2,18},{18,2},{3,19},{19,3},{4,20},{20... | collective-permute-start | bytes 786440 | tf_op jit(solution)/shard_map/ppermute | solution.py:32
  77.9 8.0 %collective-permute-start.14 = (bf16[16,32,256]{2,1,0:T(8,128)(2,1)S(1)}, bf16[16,32,256]{2,1,0:T(8,128)(2,1)S(1)}, u32[]{:S(2)}, u32[]{:S(2)}) collective-permute-start(bf16[16,32,256]{2,1,0:T(8,128)(2,1)S(1)} %collective-permute-done.5.refs_5_), channel_id=1, source_target_pairs={{0,16},{16,0},{1,17},{17,1},{2,18},{18,2},{3,19},{19,3},{4,20},{20... | collective-permute-start | bytes 786440 | tf_op jit(solution)/shard_map/ppermute | solution.py:32
  78.4 3.4 %copy-start.1 = (bf16[1024,4096]{1,0:T(8,128)(2,1)S(1)}, bf16[1024,4096]{1,0:T(8,128)(2,1)}, u32[]{:S(2)}) copy-start(bf16[1024,4096]{1,0:T(8,128)(2,1)} %acts_ref.4) | copy-start | bytes 25165828
  81.8 6.4 %collective-permute-start.15 = (bf16[16,32,256]{2,1,0:T(8,128)(2,1)S(1)}, bf16[16,32,256]{2,1,0:T(8,128)(2,1)S(1)}, u32[]{:S(2)}, u32[]{:S(2)}) collective-permute-start(bf16[16,32,256]{2,1,0:T(8,128)(2,1)S(1)} %collective-permute-done.6.refs_6_), channel_id=1, source_target_pairs={{0,16},{16,0},{1,17},{17,1},{2,18},{18,2},{3,19},{19,3},{4,20},{20... | collective-permute-start | bytes 786440 | tf_op jit(solution)/shard_map/ppermute | solution.py:32
  82.1 6.1 %collective-permute-start.16 = (bf16[16,32,256]{2,1,0:T(8,128)(2,1)S(1)}, bf16[16,32,256]{2,1,0:T(8,128)(2,1)S(1)}, u32[]{:S(2)}, u32[]{:S(2)}) collective-permute-start(bf16[16,32,256]{2,1,0:T(8,128)(2,1)S(1)} %collective-permute-done.8.refs_7_), channel_id=1, source_target_pairs={{0,16},{16,0},{1,17},{17,1},{2,18},{18,2},{3,19},{19,3},{4,20},{20... | collective-permute-start | bytes 786440 | tf_op jit(solution)/shard_map/ppermute | solution.py:32
  82.6 8.0 %collective-permute-start.17 = (bf16[4,32,512]{2,1,0:T(8,128)(2,1)S(1)}, bf16[4,32,512]{2,1,0:T(8,128)(2,1)S(1)}, u32[]{:S(2)}, u32[]{:S(2)}) collective-permute-start(bf16[4,32,512]{2,1,0:T(8,128)(2,1)S(1)} %pad_maximum_fusion.refs_0_), channel_id=1, source_target_pairs={{0,32},{32,64},{64,96},{96,0},{1,33},{33,65},{65,97},{97,1},{2,34}... | collective-permute-start | bytes 393224 | tf_op jit(solution)/shard_map/ppermute | solution.py:200
  83.2 8.3 %collective-permute-start.18 = (bf16[4,32,512]{2,1,0:T(8,128)(2,1)S(1)}, bf16[4,32,512]{2,1,0:T(8,128)(2,1)S(1)}, u32[]{:S(2)}, u32[]{:S(2)}) collective-permute-start(bf16[4,32,512]{2,1,0:T(8,128)(2,1)S(1)} %pad_maximum_fusion.refs_0_), channel_id=1, source_target_pairs={{0,96},{32,0},{64,32},{96,64},{1,97},{33,1},{65,33},{97,65},{2,98}... | collective-permute-start | bytes 393224 | tf_op jit(solution)/shard_map/ppermute | solution.py:200
  85.9 6.5 %collective-permute-start.19 = (bf16[4,32,512]{2,1,0:T(8,128)(2,1)S(1)}, bf16[4,32,512]{2,1,0:T(8,128)(2,1)S(1)}, u32[]{:S(2)}, u32[]{:S(2)}) collective-permute-start(bf16[4,32,512]{2,1,0:T(8,128)(2,1)S(1)} %pad_maximum_fusion.refs_0_), channel_id=1, source_target_pairs={{0,64},{32,96},{64,0},{96,32},{1,65},{33,97},{65,1},{97,33},{2,66}... | collective-permute-start | bytes 393224 | tf_op jit(solution)/shard_map/ppermute | solution.py:200
  88.2 4.1 %copy-start.3 = (bf16[1024,512]{1,0:T(8,128)(2,1)S(1)}, bf16[1024,512]{1,0:T(8,128)(2,1)}, u32[]{:S(2)}) copy-start(bf16[1024,512]{1,0:T(8,128)(2,1)} %grads_ref.3) | copy-start | bytes 3145732
